TPU v7x, 512 devices: a whole 4x8x8 slice. The times are simulated.
512 devices in a mesh: row: 16 (over z, core), col: 32 (over y, x).
Axes of the slice: x: 4, y: 8, z: 8, core: 2. Of those that a mesh axis runs over, the one named last changes fastest.
Arguments:
- points: float32 [32768, 128], P(('row', 'col')), may hold values from -6 to 6
- start_panel: float32 [32768, 64], P('row'), may hold values from -6 to 6
Outputs:
- panels: float32 [32768, 64], P('row')
- ritz_sum: float32 [64, 64], replicated
All inputs are finite; a program needn't handle non-finite values.
Results may differ from a plain program's by a relative error of at most 0.0075.
Values may be sent and summed in bfloat16 or wider, within the bound.
A program may use at most 64 MiB of HBM per device.

v0:
```python
import math

import jax
import jax.numpy as jnp
from jax import lax
from jax.sharding import PartitionSpec as P

PASSES = 2


sharpness = 5.0


def spread(value, axis, source):
    kept = jnp.where(lax.axis_index(axis) == source, value, 0).astype(value.dtype)
    return lax.psum(kept, axis)


def unit_rows(values):
    return (
        values
        * lax.rsqrt(jnp.mean(values * values, axis=1, keepdims=True) + 1e-06)
        / math.sqrt(values.shape[1])
    )


def affinity(left_pts, right_pts):
    inner_prod = jnp.dot(
        left_pts, right_pts.T, precision=lax.Precision.HIGHEST, preferred_element_type=jnp.float32
    )
    return jnp.exp(sharpness * (inner_prod - 1.0))


def orthonormal(gram_sum, product_rows):
    factor = jnp.linalg.cholesky(gram_sum)
    return lax.linalg.triangular_solve(
        factor, product_rows, left_side=False, lower=True, transpose_a=True
    )


def highest(left_mat, right_mat):
    return jnp.dot(
        left_mat, right_mat, precision=lax.Precision.HIGHEST, preferred_element_type=jnp.float32
    )


def local(points, start_panel):
    row_count = lax.axis_size("row")
    col_count = lax.axis_size("col")
    col_ratio = col_count // row_count
    col_index = lax.axis_index("col")
    root_row = col_index // col_ratio
    unit_points = unit_rows(points)
    row_points = lax.all_gather(unit_points, "col", axis=0, tiled=True)
    block_count = row_points.shape[0]
    col_width = block_count // col_ratio
    point_count = block_count * row_count
    offset = col_index % col_ratio * col_width
    col_points = spread(lax.dynamic_slice_in_dim(row_points, offset, col_width, 0), "row", root_row)
    first_tile = affinity(row_points, col_points)
    degrees = lax.psum(jnp.sum(first_tile, axis=1), "col")
    inv_root = lax.rsqrt(degrees)
    panels = start_panel
    ritz_sum = jnp.zeros((panels.shape[1], panels.shape[1]), jnp.float32)
    for pass_index in range(PASSES):
        scaled = (inv_root[:, None] * panels).astype(jnp.bfloat16)
        col_panel = spread(lax.dynamic_slice_in_dim(scaled, offset, col_width, 0), "row", root_row)
        product_rows = inv_root[:, None] * lax.psum(
            jnp.dot(
                affinity(row_points, col_points).astype(jnp.bfloat16),
                col_panel,
                preferred_element_type=jnp.float32,
            ),
            "col",
        )
        gram_sum, ritz_sum = lax.psum(
            (highest(product_rows.T, product_rows), highest(panels.T, product_rows)), "row"
        )
        gram_sum = gram_sum / point_count
        ritz_sum = ritz_sum / point_count
        panels = orthonormal(gram_sum, product_rows)
    return (panels, ritz_sum)


def solution(mesh):
    in_specs = (P(("row", "col"), None), P("row", None))
    out_specs = (P("row", None), P())
    return jax.shard_map(local, mesh=mesh, in_specs=in_specs, out_specs=out_specs, check_vma=False)
```

profile of v0, /device:TPU:1, one launch (start us, length us, event | category | flops | bytes accessed | tf_op | source)
XLA Modules:
  0.0 982.5 jit_solution(2116787405290606465)
XLA Ops:
  7.2 0.0 copy-start
  7.2 0.0 all-gather.2.cloned.1.call-start
  7.2 0.9 multiply_reduce_fusion
  8.1 1.5 multiply_multiply_fusion
  9.6 0.0 all-gather.2.cloned.1.call-update
  9.6 0.0 all-reduce.7.cloned.1.call-start
  9.7 84.6 %all-gather.2.cloned.1.call-done = f32[2048,128]{1,0:T(8,128)} async-done(((f32[64,128]{1,0:T(8,128)}), f32[2048,128]{1,0:T(8,128)}) %all-gather.2.cloned.1.call-update) | async-done | bytes 1048592 | tf_op jit(solution)/shard_map/all_gather | solution.py:54
  94.3 1.9 dynamic-slice_select_fusion
  96.2 0.0 all-reduce.7.cloned.1.call-update
  96.2 0.0 all-reduce.9.cloned.1.call-start
  96.3 119.2 %all-reduce.7.cloned.1.call-done = f32[1024,128]{1,0:T(8,128)} async-done(((f32[1024,128]{1,0:T(8,128)}), f32[1024,128]{1,0:T(8,128)}) %all-reduce.7.cloned.1.call-update) | async-done | bytes 524304 | tf_op jit(solution)/shard_map/psum | solution.py:16
  215.5 10.9 %fusion.1 = (f32[2048]{0:T(1024)S(1)}, f32[2048,1024]{0,1:T(8,128)}) fusion(f32[2048,128]{1,0:T(8,128)} %all-gather.2.cloned.1.call-done, f32[1024,128]{1,0:T(8,128)} %all-reduce.7.cloned.1.call-done), kind=kOutput, calls=%fused_computation.2 | convolution fusion | flops 3227514880 | bytes 9969664 | tf_op jit(solution)/shard_map/dot_general | solution.py:28
  226.4 61.4 %psum.64 = f32[2048]{0:T(1024)S(1)} all-reduce(f32[2048]{0:T(1024)S(1)} %get-tuple-element.8), channel_id=1, replica_groups=mesh['row'=16,'col'=32] {'col'}, use_global_device_ids=true, to_apply=%region_3.4 | all-reduce | flops 2048 | bytes 16384 | tf_op jit(solution)/shard_map/psum | solution.py:61
  287.8 0.0 copy-done
  287.8 0.7 fusion.21
  288.5 0.0 all-reduce.9.cloned.1.call-update
  288.5 0.0 all-reduce.11.cloned.1.call-start
  288.6 123.0 %all-reduce.9.cloned.1.call-done = bf16[1024,64]{0,1:T(8,128)(2,1)} async-done(((bf16[1024,64]{0,1:T(8,128)(2,1)}), bf16[1024,64]{0,1:T(8,128)(2,1)}) %all-reduce.9.cloned.1.call-update) | async-done | bytes 131088 | tf_op jit(solution)/shard_map/psum | solution.py:16
  411.6 5.8 fusion.2
  417.4 0.0 all-reduce.11.cloned.1.call-update
  417.4 0.0 all-reduce.13.cloned.1.call-start
  417.5 153.6 %all-reduce.11.cloned.1.call-done = f32[2048,64]{0,1:T(8,128)} async-done(((f32[2048,64]{0,1:T(8,128)}), f32[2048,64]{0,1:T(8,128)}) %all-reduce.11.cloned.1.call-update) | async-done | bytes 524304 | tf_op jit(solution)/shard_map/psum | solution.py:68
  571.1 1.8 fusion.7
  572.9 48.4 %psum.67 = f32[64,64]{0,1:T(8,128)S(1)} all-reduce(f32[64,64]{0,1:T(8,128)S(1)} %fusion.7), channel_id=1, replica_groups=mesh['row'=16,'col'=32] {'row'}, use_global_device_ids=true, to_apply=%region_6.7 | all-reduce | flops 4096 | bytes 32768 | tf_op jit(solution)/shard_map/psum | solution.py:76
  621.2 0.1 copy.5
  621.3 5.8 cholesky.44
  627.2 0.6 compare_reduce_fusion.1
  627.9 0.7 fusion.23
  628.5 4.9 custom-call.6
  633.4 1.7 convolution_bitcast_fusion.1
  635.1 0.7 fusion.22
  635.8 0.0 all-reduce.13.cloned.1.call-update
  635.8 0.0 all-reduce.15.cloned.1.call-start
  635.9 113.0 %all-reduce.13.cloned.1.call-done = bf16[1024,64]{0,1:T(8,128)(2,1)} async-done(((bf16[1024,64]{0,1:T(8,128)(2,1)}), bf16[1024,64]{0,1:T(8,128)(2,1)}) %all-reduce.13.cloned.1.call-update) | async-done | bytes 131088 | tf_op jit(solution)/shard_map/psum | solution.py:16
  748.9 5.8 fusion.4
  754.7 0.0 all-reduce.15.cloned.1.call-update
  754.7 153.7 %all-reduce.15.cloned.1.call-done = f32[2048,64]{0,1:T(8,128)} async-done(((f32[2048,64]{0,1:T(8,128)}), f32[2048,64]{0,1:T(8,128)}) %all-reduce.15.cloned.1.call-update) | async-done | bytes 524304 | tf_op jit(solution)/shard_map/psum | solution.py:68
  908.4 1.6 fusion.9
  910.0 1.8 fusion.12
  911.8 48.5 %all-reduce = (f32[64,64]{0,1:T(8,128)S(1)}, f32[64,64]{0,1:T(8,128)S(1)}) all-reduce(f32[64,64]{0,1:T(8,128)S(1)} %fusion.12, f32[64,64]{0,1:T(8,128)S(1)} %fusion.9), channel_id=1, replica_groups=mesh['row'=16,'col'=32] {'row'}, use_global_device_ids=true, to_apply=%region_11.14 | all-reduce | flops 8192 | bytes 65536 | tf_op jit(solution)/shard_map/psum | solution.py:76
  960.3 0.7 copy.9
  961.0 0.1 copy.7
  961.1 5.8 cholesky.55
  967.0 0.6 compare_reduce_fusion
  967.6 0.7 fusion.24
  968.3 4.9 custom-call.7
  973.2 2.5 convolution_bitcast_fusion
  (9 shorter events, 0.1 us)
Async XLA Ops:
  7.2 280.7 %copy-start = (f32[2048,64]{0,1:T(8,128)S(1)}, f32[2048,64]{0,1:T(8,128)}, u32[]{:S(2)}) copy-start(f32[2048,64]{0,1:T(8,128)} %param.6) | copy-start | bytes 1572868
  7.2 87.1 %all-gather.2.cloned.1.call-start = ((), (), s32[]{:S(2)}) async-start(), calls=%async_computation | async-start | bytes 1081344 | tf_op jit(solution)/shard_map/all_gather | solution.py:54
  9.6 205.8 %all-reduce.7.cloned.1.call-start = ((), (), s32[]{:S(2)}) async-start(), calls=%async_computation.1 | async-start | bytes 1048576 | tf_op jit(solution)/shard_map/psum | solution.py:16
  96.2 315.4 %all-reduce.9.cloned.1.call-start = ((), (), s32[]{:S(2)}) async-start(), calls=%async_computation.2 | async-start | bytes 262144 | tf_op jit(solution)/shard_map/psum | solution.py:16
  288.5 282.5 %all-reduce.11.cloned.1.call-start = ((), (), s32[]{:S(2)}) async-start(), calls=%async_computation.3 | async-start | bytes 1048576 | tf_op jit(solution)/shard_map/psum | solution.py:68
  417.4 331.5 %all-reduce.13.cloned.1.call-start = ((), (), s32[]{:S(2)}) async-start(), calls=%async_computation.4 | async-start | bytes 262144 | tf_op jit(solution)/shard_map/psum | solution.py:16
  635.8 272.6 %all-reduce.15.cloned.1.call-start = ((), (), s32[]{:S(2)}) async-start(), calls=%async_computation.5 | async-start | bytes 1048576 | tf_op jit(solution)/shard_map/psum | solution.py:68
Sparse Core Ops, SparseCore 0:
  11.7 82.5 all-gather.1
  97.2 118.2 all-reduce.6
  288.7 122.9 all-reduce.8
  417.5 153.4 all-reduce.10
  636.0 112.8 all-reduce.12
  754.8 153.5 all-reduce.14
where the time goes:
time: 984 us; the launch traced here: 982 us
  waiting for transfers between devices  747 us (76%)
  blocking collectives  158 us (16%)
  matrix products  31.8 us (3%)
  other arithmetic  29.8 us (3%)
  between operations  14.3 us (1%)
    psum x3, waiting for transfers between devices, spread(): return lax.psum(kept, axis)  355 us
    psum x2, waiting for transfers between devices, local(): lax.psum(jnp.dot(affinity(row_points, col_points).astype(jnp.bfloat16), c...  307 us
    psum x2, blocking collectives, local(): lax.psum((highest(product_rows.T, product_rows), highest(panels.T, produc...  96.8 us
    all_gather x1, waiting for transfers between devices, local(): row_points = lax.all_gather(unit_points, 'col', axis=0, tiled=True)  84.6 us
    psum x1, blocking collectives, local(): degrees = lax.psum(jnp.sum(first_tile, axis=1), 'col')  61.4 us
  transfers between devices with their start and end apart: 6, of which 6 were waited for; matrix products, arithmetic and copies ran while one was open for 0% of the time, Pallas kernels for 0%

commit v1 on v0

v1 whole, which is shorter than its diff:
```python
import functools
import math

import jax
import jax.numpy as jnp
from jax import lax
from jax.experimental import pallas as pl
from jax.experimental.pallas import tpu as pltpu
from jax.sharding import PartitionSpec as P

MESH = pl.DeviceIdType.MESH
NX = 4
HALF = 32
SHARPNESS = 5.0
LOG2E = math.log2(math.e)
f32 = jnp.float32
bf16 = jnp.bfloat16


def dot(a, b, contract=((1,), (0,)), precision=None):
    return lax.dot_general(
        a, b, (contract, ((), ())), precision=precision, preferred_element_type=f32
    )


def full(a, b, contract=((1,), (0,))):
    return dot(a, b, contract, lax.Precision.HIGHEST)


def inverse_factor(gram):
    n = gram.shape[0]
    rows = lax.broadcasted_iota(jnp.int32, (n, 2 * n), 0)
    lanes = lax.broadcasted_iota(jnp.int32, (n, 2 * n), 1)
    sub = lax.broadcasted_iota(jnp.int32, (n, 1), 0)
    eye = jnp.where(rows[:, :n] == lanes[:, :n], 1.0, 0.0).astype(f32)

    def step(k, carry):
        mat, diag = carry
        col = jnp.sum(jnp.where(lanes == k, mat, 0.0), axis=1, keepdims=True)
        row = jnp.sum(jnp.where(rows == k, mat, 0.0), axis=0, keepdims=True)
        pivot = jnp.sum(jnp.where(sub == k, col, 0.0), axis=0, keepdims=True)
        mat = mat - jnp.where(sub > k, col / pivot, 0.0) * row
        return mat, jnp.where(sub == k, pivot, diag)

    start = (jnp.concatenate([gram, eye], axis=1), jnp.ones((n, 1), f32))
    mat, diag = lax.fori_loop(0, n, step, start)
    return mat[:, n:] * lax.rsqrt(diag)


def pack(mat):
    n = mat.shape[0] // 2
    return jnp.concatenate([mat[:n], mat[n:]], axis=1)


def unpack(mat):
    n = mat.shape[1] // 2
    return jnp.concatenate([mat[:, :n], mat[:, n:]], axis=0)


def kernel(
    nz, ny, points_ref, start_ref, out_ref, ritz_ref,
    rowpts, colpts, tile, startT, scaledT, deg, deg_x, deg_y, turn,
    half_c, recv_c, send_z, recv_z, scaled, send_p, recv_px, send_y, recv_py,
    gram, gram_x, gram_y, gram_c, gram_z, whole, send_sem, recv_sem,
):
    r, c = lax.axis_index("row"), lax.axis_index("col")
    z, core = r // 2, lax.rem(r, 2)
    y, x = c // NX, lax.rem(c, NX)
    axes = {
        "x": (NX, x, lambda p: (r, y * NX + p)),
        "y": (ny, y, lambda p: (r, p * NX + x)),
        "z": (nz, z, lambda p: (p * 2 + core, c)),
        "c": (2, core, lambda p: (z * 2 + p, c)),
    }
    count = (NX - 1) + (ny - 1) + (nz - 1) + 1
    total = nz * ny * NX * 2 * 2 * HALF

    barrier = pltpu.get_barrier_semaphore()
    for n, me, device in axes.values():
        def greet(i, carry):
            pl.semaphore_signal(
                barrier, inc=1, device_id=device(lax.rem(me + i, n)), device_id_type=MESH
            )
            return carry
        lax.fori_loop(1, n, greet, 0)

    sent = []

    def send(slot, axis, src, dst):
        n, me, device = axes[axis]

        def one(i, carry):
            p = lax.rem(me + i, n)
            pltpu.make_async_remote_copy(
                src_ref=src(p), dst_ref=dst, send_sem=send_sem.at[slot],
                recv_sem=recv_sem.at[slot], device_id=device(p), device_id_type=MESH,
            ).start()
            return carry
        lax.fori_loop(1, n, one, 0)

    def arrive(slot, ref):
        pltpu.make_async_copy(ref, ref, recv_sem.at[slot]).wait()
        sent.append((slot, ref))

    def all_sum(slot, axis, value, buf):
        n, me, _ = axes[axis]
        buf[me] = value
        send(slot, axis, lambda p: buf.at[me], buf.at[me])
        def done():
            arrive(slot, buf.at[pl.ds(0, n - 1)])
            return functools.reduce(lambda a, b: a + b, [buf[i] for i in range(n)])
        return done

    pts = points_ref[...]
    width = pts.shape[1]
    unit = pts * lax.rsqrt(jnp.mean(pts * pts, axis=1, keepdims=True) + 1e-06)
    unit = unit * math.sqrt(SHARPNESS * LOG2E / width)
    unit = unit.astype(bf16).reshape(2, HALF, width)
    rowpts[:, y, x] = unit
    colpts[core, :, z] = unit

    pl.semaphore_wait(barrier, count)

    send(0, "y", lambda p: rowpts.at[:, y, x], rowpts.at[:, y, x])
    send(1, "z", lambda p: colpts.at[core, :, z], colpts.at[core, :, z])

    def turn_start(t, carry):
        h, yy = t // ny, lax.rem(t, ny)
        part = start_ref[yy, :, h]
        startT[t] = part.reshape(NX * HALF, part.shape[2]).T
        return carry
    lax.fori_loop(0, 2 * ny, turn_start, 0)

    arrive(0, rowpts.at[:, pl.ds(0, ny - 1), 0])
    send(2, "x", lambda p: rowpts.at[:, :, x], rowpts.at[:, :, x])
    arrive(1, colpts.at[0, :, pl.ds(0, nz - 1)])
    send(3, "c", lambda p: colpts.at[core], colpts.at[core])
    arrive(2, rowpts.at[:, :, pl.ds(0, NX - 1)])
    arrive(3, colpts.at[0])

    ncols = 4 * nz * HALF
    wide = NX * HALF
    ones = jnp.ones((8, wide), f32)
    shift = SHARPNESS * LOG2E

    def affinity(t, carry):
        h, yy = t // ny, lax.rem(t, ny)
        left = rowpts[h, yy].reshape(wide, width)
        right = colpts[...].reshape(ncols, width)
        value = jnp.exp2(dot(left, right, ((1,), (1,))) - shift)
        tile[h, yy] = value.astype(bf16)
        part = value[:, :128]
        for j in range(1, ncols // 128):
            part = part + value[:, j * 128:(j + 1) * 128]
        sums = full(ones, part, ((1,), (1,)))
        deg[pl.ds(t, 1), :] = sums[:1]
        return carry
    lax.fori_loop(0, 2 * ny, affinity, 0)

    degrees = all_sum(4, "x", deg[...], deg_x)()
    degrees = all_sum(5, "y", degrees, deg_y)()
    inv_root = lax.rsqrt(degrees)
    deg[...] = inv_root
    for h in range(2):
        line = deg[pl.ds(h * ny + y, 1), :]
        turn[h] = jnp.broadcast_to(line, (wide, wide)).T
    low = lax.broadcasted_iota(jnp.int32, (HALF, 4 * HALF), 1) < 2 * HALF
    mine = pl.ds(x * HALF, HALF)
    inv_packed = jnp.where(low, turn[0, mine, :2 * 2 * HALF], turn[1, mine, :2 * 2 * HALF])

    for t in range(2 * ny):
        scaledT[:, t * wide:(t + 1) * wide] = (startT[t] * inv_root[t:t + 1]).astype(bf16)
    for k in range(2):
        part = tile[...].reshape(2 * ny * wide, ncols)[:, k * ncols // 2:(k + 1) * ncols // 2]
        half_c[k] = dot(scaledT[...], part)
    send(6, "c", lambda p: half_c.at[p], recv_c)
    arrive(6, recv_c)
    both = half_c[core] + recv_c[...]
    mid = both.shape[1] // 2
    both = jnp.concatenate([both[:, :mid], both[:, mid:]], axis=0).T
    send_z[...] = both.reshape(send_z.shape)
    send(7, "z", lambda p: send_z.at[p], recv_z.at[z])
    recv_z[z] = send_z[z]
    arrive(7, recv_z.at[pl.ds(0, nz - 1)])
    panel = functools.reduce(lambda a, b: a + b, [recv_z[i] for i in range(nz)])
    first_packed = panel * inv_packed
    first = unpack(first_packed)

    second_in = unpack(first_packed * inv_packed)
    high = second_in.astype(bf16)
    rest = (second_in - high.astype(f32)).astype(bf16)
    scaled[core, :, z] = jnp.concatenate([high, rest], axis=1).reshape(2, HALF, -1)
    send(8, "z", lambda p: scaled.at[core, :, z], scaled.at[core, :, z])
    gram_sum = pack(full(first.T, first))
    sum_x = all_sum(9, "x", gram_sum, gram_x.at[0])
    arrive(8, scaled.at[0, :, pl.ds(0, nz - 1)])
    send(10, "c", lambda p: scaled.at[core], scaled.at[core])
    sum_y = all_sum(11, "y", sum_x(), gram_y.at[0])
    arrive(10, scaled.at[0])

    lane = lax.broadcasted_iota(jnp.int32, (wide, 4 * HALF), 1) < 2 * HALF

    def product(yy, carry):
        panel_in = scaled[...].reshape(ncols, 4 * HALF)
        parts = []
        for h in range(2):
            out = dot(tile[h, yy], panel_in)
            parts.append(out + pltpu.roll(out, 2 * HALF, 1))
        send_p[yy] = jnp.where(lane, parts[0], parts[1]).reshape(NX, HALF, 4 * HALF)
        return carry
    lax.fori_loop(0, ny, product, 0)
    send(12, "x", lambda p: send_p.at[:, p], recv_px.at[x])
    recv_px[x] = send_p[:, x]
    sum_c = all_sum(13, "c", sum_y(), gram_c.at[0])
    sum_z = all_sum(14, "z", sum_c(), gram_z.at[0])
    arrive(12, recv_px.at[pl.ds(0, NX - 1)])
    send_y[...] = functools.reduce(lambda a, b: a + b, [recv_px[i] for i in range(NX)])
    send(15, "y", lambda p: send_y.at[p], recv_py.at[y])
    recv_py[y] = send_y[y]
    inv_first = inverse_factor(unpack(sum_z()) / total)
    arrive(15, recv_py.at[pl.ds(0, ny - 1)])
    panel = functools.reduce(lambda a, b: a + b, [recv_py[i] for i in range(ny)])
    second = full(unpack(panel * inv_packed), inv_first, ((1,), (1,)))
    basis = full(first, inv_first, ((1,), (1,)))

    whole[y, x] = pack(second)
    n = second.shape[1]
    sums = jnp.concatenate([full(second.T, second), full(basis.T, second)], axis=1)
    sum_x = all_sum(16, "x", sums, gram.at[0])
    send(17, "y", lambda p: whole.at[y, x], whole.at[y, x])
    sum_y = all_sum(18, "y", sum_x(), gram.at[1])
    arrive(17, whole.at[pl.ds(0, ny - 1), 0])
    send(19, "x", lambda p: whole.at[:, x], whole.at[:, x])
    sum_c = all_sum(20, "c", sum_y(), gram.at[2])
    sum_z = all_sum(21, "z", sum_c(), gram.at[3])
    sums = sum_z() / total
    ritz_ref[...] = sums[:, n:]
    last = inverse_factor(sums[:, :n]).T
    none = jnp.zeros_like(last)
    last = jnp.concatenate(
        [jnp.concatenate([last, none], axis=0), jnp.concatenate([none, last], axis=0)], axis=1
    )
    arrive(19, whole.at[:, pl.ds(0, NX - 1)])

    def finish(yy, carry):
        block = full(whole[yy].reshape(wide, 4 * HALF), last)
        for h in range(2):
            out_ref[yy, :, h] = block[:, h * n:(h + 1) * n].reshape(NX, HALF, n)
        return carry
    lax.fori_loop(0, ny, finish, 0)

    for slot, ref in sent:
        pltpu.make_async_copy(ref, ref, send_sem.at[slot]).wait()


def local(points, start_panel):
    nz = lax.axis_size("row") // 2
    ny = lax.axis_size("col") // NX
    rows, vec = start_panel.shape
    width = points.shape[1]
    wide = NX * HALF
    lanes = 2 * vec
    ncols = 4 * nz * HALF
    vmem = pltpu.VMEM
    panels, ritz_sum = pl.pallas_call(
        functools.partial(kernel, nz, ny),
        out_shape=(
            jax.ShapeDtypeStruct((ny, NX, 2, HALF, vec), f32),
            jax.ShapeDtypeStruct((vec, vec), f32),
        ),
        in_specs=[pl.BlockSpec(memory_space=vmem)] * 2,
        out_specs=(pl.BlockSpec(memory_space=vmem),) * 2,
        scratch_shapes=[
            vmem((2, ny, NX, HALF, width), bf16),
            vmem((2, 2, nz, HALF, width), bf16),
            vmem((2, ny, wide, ncols), bf16),
            vmem((2 * ny, vec, wide), f32),
            vmem((vec, 2 * ny * wide), bf16),
            vmem((2 * ny, wide), f32),
            vmem((NX, 2 * ny, wide), f32),
            vmem((ny, 2 * ny, wide), f32),
            vmem((2, wide, wide), f32),
            vmem((2, vec, ncols // 2), f32),
            vmem((vec, ncols // 2), f32),
            vmem((nz, HALF, lanes), f32),
            vmem((nz, HALF, lanes), f32),
            vmem((2, 2, nz, HALF, lanes), bf16),
            vmem((ny, NX, HALF, lanes), f32),
            vmem((NX, ny, HALF, lanes), f32),
            vmem((ny, HALF, lanes), f32),
            vmem((ny, HALF, lanes), f32),
            vmem((4, max(nz, ny, NX), vec, lanes), f32),
            vmem((1, NX, vec // 2, lanes), f32),
            vmem((1, ny, vec // 2, lanes), f32),
            vmem((1, 2, vec // 2, lanes), f32),
            vmem((1, nz, vec // 2, lanes), f32),
            vmem((ny, NX, HALF, lanes), f32),
            pltpu.SemaphoreType.DMA((22,)),
            pltpu.SemaphoreType.DMA((22,)),
        ],
        compiler_params=pltpu.CompilerParams(
            collective_id=0, has_side_effects=True, vmem_limit_bytes=40 << 20
        ),
        name="embed",
    )(points, start_panel.reshape(ny, NX, 2, HALF, vec))
    return panels.reshape(rows, vec), ritz_sum


def solution(mesh):
    in_specs = (P(("row", "col"), None), P("row", None))
    out_specs = (P("row", None), P())
    return jax.shard_map(local, mesh=mesh, in_specs=in_specs, out_specs=out_specs, check_vma=False)
```

time: 984 us -> 116 us (0.12)
  waiting for transfers between devices: 747 us -> 0 us
  blocking collectives: 158 us -> 0 us
  Pallas kernels: 0 us -> 112 us
  matrix products: 31.8 us -> 0 us
  other arithmetic: 29.8 us -> 0 us
  between operations: 14.3 us -> 0.66 us
    psum x5 -> x0, waiting for transfers between devices: 663 us -> none  [the longest x3 355 us: spread(): return lax.psum(kept, axis)]
    psum x3 -> x0, blocking collectives: 158 us -> none  [the longest x2 96.8 us: local(): lax.psum((highest(product_rows.T, product_rows), highest(panels.T, produc...]
    pallas_call x0 -> x1, Pallas kernels: none -> 112 us  [local(): pl.pallas_call(functools.partial(kernel, nz, ny), out_shape=(jax.ShapeDty...]
    all_gather x1 -> x0, waiting for transfers between devices: 84.6 us -> none  [local(): row_points = lax.all_gather(unit_points, 'col', axis=0, tiled=True)]
    dot_general x6 -> x0, matrix products: 27.7 us -> none  [the longest x2 11.5 us: local(): jnp.dot(affinity(row_points, col_points).astype(jnp.bfloat16), col_panel,...]
    another operation x10 -> x0, other arithmetic: 24.1 us -> none  [the longest x6 13 us: orthonormal(): factor = jnp.linalg.cholesky(gram_sum)]
  transfers between devices with their start and end apart: 6 -> 0, of which waited for: 6 -> 0; matrix products, arithmetic and copies ran while one was open for 0% -> 0% of each run, Pallas kernels for 0% -> 0%
where the time goes in v1:
time: 116 us
  Pallas kernels  112 us (97%)
  local copies, waits for them, and re-layouts  3.11 us (3%)
    pallas_call x1, Pallas kernels, local(): pl.pallas_call(functools.partial(kernel, nz, ny), out_shape=(jax.ShapeDty...  112 us
    unnamed x5, local copies, waits for them, and re-layouts  3.11 us

profile of v1, /device:TPU:1, one launch (start us, length us, event | category | flops | bytes accessed | tf_op | source)
XLA Modules:
  0.0 115.6 jit_solution(15947164847951144447)
XLA Ops:
  0.6 0.0 copy-start
  0.6 1.4 %copy.4 = f32[2048,64]{1,0:T(8,128)S(1)} copy(f32[2048,64]{0,1:T(8,128)} %param.3) | data formatting | bytes 1048576 | tf_op args[1]
  2.0 0.0 copy-done
  2.0 111.8 %embed.1 = (f32[8,4,2,32,64]{4,3,2,1,0:T(8,128)S(1)}, f32[64,64]{1,0:T(8,128)S(1)}) custom-call(f32[64,128]{1,0:T(8,128)S(1)} %copy-done, f32[8,4,2,32,64]{4,3,2,1,0:T(8,128)S(1)} %bitcast.2), custom_call_target="tpu_custom_call" | custom-call | tf_op jit(solution)/shard_map/embed/pallas_call | solution.py:265
  113.9 1.1 copy.5
  115.0 0.6 copy.7
Async XLA Ops:
  0.6 1.4 %copy-start = (f32[64,128]{1,0:T(8,128)S(1)}, f32[64,128]{1,0:T(8,128)}, u32[]{:S(2)}) copy-start(f32[64,128]{1,0:T(8,128)} %points_ref.1) | copy-start | bytes 98308

commit v2 on v0

v2 whole, which is shorter than its diff:
```python
import functools
import math

import jax
import jax.numpy as jnp
from jax import lax
from jax.experimental import pallas as pl
from jax.experimental.pallas import tpu as pltpu
from jax.sharding import PartitionSpec as P

MESH = pl.DeviceIdType.MESH
NX = 4
HALF = 32
OWN = 2 * HALF
LANES = 128
SHARPNESS = 5.0
LOG2E = math.log2(math.e)
f32 = jnp.float32
bf16 = jnp.bfloat16


def dot(a, b, contract=((1,), (0,)), precision=None):
    return lax.dot_general(
        a, b, (contract, ((), ())), precision=precision, preferred_element_type=f32
    )


def full(a, b, contract=((1,), (0,))):
    return dot(a, b, contract, lax.Precision.HIGHEST)


def iota(shape, axis):
    return lax.broadcasted_iota(jnp.int32, shape, axis)


def add(parts):
    return functools.reduce(lambda a, b: a + b, parts)


def inverse_factor(gram, width=16):
    n = gram.shape[0]
    eye = jnp.where(iota((n, n), 0) == iota((n, n), 1), 1.0, 0.0).astype(f32)
    mat = jnp.concatenate([gram, eye], axis=1)
    done = []
    for b in range(0, n, width):
        m = n - b
        cols = [jnp.broadcast_to(mat[:, b + j:b + j + 1], (m, 2 * n)) for j in range(width)]
        rows = [mat[j:j + 1] for j in range(width)]
        for j in range(width):
            root = lax.rsqrt(cols[j][j:j + 1])
            cols[j], rows[j] = cols[j] * root, rows[j] * root
            for i in range(j + 1, width):
                factor = cols[j][i:i + 1]
                cols[i], rows[i] = cols[i] - factor * cols[j], rows[i] - factor * rows[j]
        done += rows
        mat = mat[width:]
        for j in range(width if m > width else 0):
            mat = mat - cols[j][width:] * rows[j]
    return jnp.concatenate(done, axis=0)[:, n:]


def pack(mat):
    n = mat.shape[0] // 2
    return jnp.concatenate([mat[:n], mat[n:]], axis=1)


def unpack(mat):
    n = mat.shape[1] // 2
    return jnp.concatenate([mat[:, :n], mat[:, n:]], axis=0)


def kernel(
    nz, ny, points_ref, start_ref, out_ref, ritz_ref,
    startT, rowpts, colpts, tile, partial, scaledT, deg, deg_x, deg_y, turn,
    half_c, recv_c, send_z, recv_z, scaled, send_p, recv_px, send_y, recv_py,
    first_x, first_y, first_c, first_z, gram_x, gram_y, gram_c, gram_z,
    ritz_x, ritz_y, ritz_c, ritz_z, whole,
    load_sem, send_sem, recv_sem, from_y, from_x, part_x,
):
    r, c = lax.axis_index("row"), lax.axis_index("col")
    z, core = r // 2, lax.rem(r, 2)
    y, x = c // NX, lax.rem(c, NX)
    axes = {
        "x": (NX, x, lambda p: (r, y * NX + p)),
        "y": (ny, y, lambda p: (r, p * NX + x)),
        "z": (nz, z, lambda p: (p * 2 + core, c)),
        "c": (2, core, lambda p: (z * 2 + p, c)),
    }
    count = (NX - 1) + (ny - 1) + (nz - 1) + 1
    total = nz * ny * NX * 2 * OWN
    chunk = NX * OWN
    lines = chunk // LANES
    ncols = 2 * nz * OWN
    width = points_ref.shape[1]
    vec = ritz_ref.shape[0]

    load = pltpu.make_async_copy(start_ref, startT, load_sem)
    load.start()
    barrier = pltpu.get_barrier_semaphore()
    for n, me, device in axes.values():
        def greet(i, carry):
            pl.semaphore_signal(
                barrier, inc=1, device_id=device(lax.rem(me + i, n)), device_id_type=MESH
            )
            return carry
        lax.fori_loop(1, n, greet, 0)

    sent = {}
    pending = {}

    def send(slot, axis, src, dst, got, recv=None):
        n, me, device = axes[axis]
        arrival = recv_sem.at[slot] if recv is None else recv

        def one(i, carry):
            p = lax.rem(me + i, n)
            pltpu.make_async_remote_copy(
                src_ref=src(p), dst_ref=dst, send_sem=send_sem.at[slot],
                recv_sem=arrival, device_id=device(p), device_id_type=MESH,
            ).start()
            return carry
        lax.fori_loop(1, n, one, 0)
        sent[slot] = got
        if recv is None:
            pending[slot] = got

    def wait(ref, sem):
        pltpu.make_async_copy(ref, ref, sem).wait()

    def arrive(slot):
        wait(pending.pop(slot), recv_sem.at[slot])

    def drain():
        for slot in list(pending):
            arrive(slot)
        for slot, ref in sent.items():
            wait(ref, send_sem.at[slot])

    def all_sum(slot, axis, value, buf):
        n, me, _ = axes[axis]
        buf[me] = value
        send(slot, axis, lambda p: buf.at[me], buf.at[me], buf.at[pl.ds(0, n - 1)])

        def done():
            arrive(slot)
            return add([buf[i] for i in range(n)])
        return done

    def near(i):
        return lax.rem(y + 2 * ny + (2 * lax.rem(i, 2) - 1) * ((i + 1) // 2), ny)

    shift = SHARPNESS * LOG2E
    pts = points_ref[...]
    unit = pts * lax.rsqrt(jnp.mean(pts * pts, axis=1, keepdims=True) + 1e-06)
    unit = (unit * math.sqrt(shift / width)).astype(bf16)
    rowpts[y, x] = unit
    colpts[core, :, z] = unit.reshape(2, HALF, width)

    pl.semaphore_wait(barrier, count)
    send(0, "y", lambda p: rowpts.at[y, x], rowpts.at[y, x],
         rowpts.at[pl.ds(0, ny - 1), 0], from_y.at[y])
    send(1, "z", lambda p: colpts.at[core, :, z], colpts.at[core, :, z],
         colpts.at[0, :, pl.ds(0, nz - 1)])

    def forward(i, carry):
        yy = near(i)

        @pl.when(i > 0)
        def _():
            wait(rowpts.at[yy, x], from_y.at[yy])
        send(2, "x", lambda p: rowpts.at[yy, x], rowpts.at[yy, x],
             rowpts.at[:, pl.ds(0, NX - 1)], from_x.at[yy])
        return carry
    lax.fori_loop(0, ny, forward, 0)
    sent[2] = rowpts.at[:, pl.ds(0, NX - 1)]
    arrive(1)
    send(3, "c", lambda p: colpts.at[core], colpts.at[core], colpts.at[0])

    def affinity(yy, k):
        left = rowpts[yy].reshape(chunk, width)
        right = colpts[k].reshape(ncols // 2, width)
        value = jnp.exp2(dot(left, right, ((1,), (1,))) - shift)
        tile[k, yy] = value.astype(bf16)
        return add([value[:, j:j + LANES] for j in range(0, ncols // 2, LANES)])

    def near_half(i, carry):
        yy = near(i)
        wait(rowpts.at[yy, pl.ds(0, NX - 1)], from_x.at[yy])
        partial[yy] = affinity(yy, core)
        return carry
    lax.fori_loop(0, ny, near_half, 0)
    arrive(3)

    def far_half(i, carry):
        for b in range(pair):
            yy = pair * i + b
            part = partial[yy] + affinity(yy, 1 - core)
            for h in range(lines):
                deg[pl.ds(yy * lines + h, 1), :] = jnp.sum(
                    part[h * LANES:(h + 1) * LANES].T, axis=0, keepdims=True
                )
        return carry
    pair = 2 if ny % 2 == 0 else 1
    lax.fori_loop(0, ny // pair, far_half, 0)
    degrees = all_sum(4, "x", deg[...], deg_x)()
    degrees = all_sum(5, "y", degrees, deg_y)()
    inv_root = lax.rsqrt(degrees)
    deg[...] = inv_root
    load.wait()
    for t in range(ny * chunk // LANES):
        here = slice(t * LANES, (t + 1) * LANES)
        scaledT[:, here] = (startT[:, here] * inv_root[t:t + 1]).astype(bf16)

    def transposed(k):
        half_c[k] = dot(scaledT[...], tile[k].reshape(ny * chunk, ncols // 2))
    transposed(1 - core)
    send(6, "c", lambda p: half_c.at[p], recv_c, recv_c)
    transposed(core)
    odd = lax.rem(x, 2)
    line = pl.ds(y * lines + x // 2, 1)
    turn[...] = jnp.broadcast_to(deg[line, :], (LANES, LANES)).T
    low = iota((HALF, LANES), 1) < vec
    inv_packed = jnp.where(
        low, turn[pl.ds(odd * OWN, HALF)], turn[pl.ds(odd * OWN + HALF, HALF)]
    )
    arrive(6)
    both = half_c[core] + recv_c[...]
    mid = both.shape[1] // 2
    both = jnp.concatenate([both[:, :mid], both[:, mid:]], axis=0).T
    send_z[...] = both.reshape(send_z.shape)
    send(7, "z", lambda p: send_z.at[p], recv_z.at[z], recv_z.at[pl.ds(0, nz - 1)])
    recv_z[z] = send_z[z]
    arrive(7)
    first_packed = add([recv_z[i] for i in range(nz)]) * inv_packed

    second_in = unpack(first_packed * inv_packed)
    high = second_in.astype(bf16)
    rest = (second_in - high.astype(f32)).astype(bf16)
    scaled[core, :, z] = jnp.concatenate([high, rest], axis=1).reshape(2, HALF, LANES)
    send(8, "z", lambda p: scaled.at[core, :, z], scaled.at[core, :, z],
         scaled.at[0, :, pl.ds(0, nz - 1)])
    first = unpack(first_packed)
    first_sum = all_sum(13, "c", pack(full(first, first, ((0,), (0,)))), first_c)
    first_sum = all_sum(9, "x", first_sum(), first_x)
    first_sum = all_sum(10, "y", first_sum(), first_y)
    arrive(8)
    send(11, "c", lambda p: scaled.at[core], scaled.at[core], scaled.at[0])

    def product(yy, k):
        return dot(tile[k, yy], scaled[k].reshape(ncols // 2, LANES))

    def near_product(i, carry):
        for b in range(pair):
            partial[pair * i + b] = product(pair * i + b, core)
        return carry
    lax.fori_loop(0, ny // pair, near_product, 0)
    arrive(11)
    keep = iota((HALF, LANES), 1) < vec

    def far_product(j, carry):
        yy = near(ny - 1 - j)
        out = partial[yy] + product(yy, 1 - core)
        out = out + pltpu.roll(out, vec, 1)
        for s in range(NX):
            send_p[yy, s] = jnp.where(
                keep, out[s * OWN:s * OWN + HALF], out[s * OWN + HALF:(s + 1) * OWN]
            )
        send(12, "x", lambda p: send_p.at[yy, p], recv_px.at[yy, x],
             send_p.at[:, pl.ds(0, NX - 1)], part_x.at[yy])
        recv_px[yy, x] = send_p[yy, x]
        return carry
    lax.fori_loop(0, ny, far_product, 0)
    sent[12] = send_p.at[:, pl.ds(0, NX - 1)]
    first_sum = all_sum(14, "z", first_sum(), first_z)

    def collect(j, carry):
        yy = near(ny - 1 - j)
        wait(recv_px.at[yy, pl.ds(0, NX - 1)], part_x.at[yy])
        send_y[yy] = add([recv_px[yy, i] for i in range(NX)])

        @pl.when(j < ny - 1)
        def _():
            pltpu.make_async_remote_copy(
                src_ref=send_y.at[yy], dst_ref=recv_py.at[y], send_sem=send_sem.at[15],
                recv_sem=recv_sem.at[15], device_id=(r, yy * NX + x), device_id_type=MESH,
            ).start()
        return carry
    lax.fori_loop(0, ny, collect, 0)
    sent[15] = pending[15] = recv_py.at[pl.ds(0, ny - 1)]
    recv_py[y] = send_y[y]
    inv_first = inverse_factor(unpack(first_sum()) / total)
    basis = full(first, inv_first, ((1,), (1,)))
    arrive(15)
    second_packed = add([recv_py[i] for i in range(ny)]) * inv_packed
    second = full(unpack(second_packed), inv_first, ((1,), (1,)))

    whole[y, x] = pack(second)
    gram = all_sum(16, "x", pack(full(second.T, second)), gram_x)
    ritz = all_sum(17, "x", pack(full(basis.T, second)), ritz_x)
    gram = all_sum(18, "y", gram(), gram_y)
    ritz = all_sum(19, "y", ritz(), ritz_y)
    send(20, "y", lambda p: whole.at[y, x], whole.at[y, x], whole.at[pl.ds(0, ny - 1), 0])
    gram = all_sum(21, "c", gram(), gram_c)
    gram = all_sum(22, "z", gram(), gram_z)
    ritz = all_sum(23, "c", ritz(), ritz_c)
    ritz = all_sum(24, "z", ritz(), ritz_z)
    arrive(20)
    send(25, "x", lambda p: whole.at[:, x], whole.at[:, x], whole.at[:, pl.ds(0, NX - 1)])
    gram = unpack(gram()) / total
    last = inverse_factor(gram)
    last = jnp.concatenate([last, jnp.zeros_like(last)], axis=1)
    arrive(25)

    group = 4 if ny % 4 == 0 else 1

    def finish(t, carry):
        parts = []
        for s in range(group * NX):
            block = whole[t * group + s // NX, s % NX]
            parts += [block, pltpu.roll(block, vec, 1)]
        here = pl.ds(pl.multiple_of(t * group * chunk, group * chunk), group * chunk)
        out_ref[:, here] = full(last, jnp.concatenate(parts, axis=0), ((1,), (1,)))
        return carry
    lax.fori_loop(0, ny // group, finish, 0)
    ritz_ref[...] = unpack(ritz()) / total
    drain()


def local(points, start_panel):
    nz = lax.axis_size("row") // 2
    ny = lax.axis_size("col") // NX
    rows, vec = start_panel.shape
    width = points.shape[1]
    chunk = NX * OWN
    lines = rows // LANES
    ncols = 2 * nz * OWN
    vmem = pltpu.VMEM
    dma = pltpu.SemaphoreType.DMA
    sums = [vmem((n, vec // 2, 2 * vec), f32) for n in (NX, ny, 2, nz)]
    panels, ritz_sum = pl.pallas_call(
        functools.partial(kernel, nz, ny),
        out_shape=(
            jax.ShapeDtypeStruct((vec, rows), f32),
            jax.ShapeDtypeStruct((vec, vec), f32),
        ),
        in_specs=[pl.BlockSpec(memory_space=vmem), pl.BlockSpec(memory_space=pl.ANY)],
        out_specs=(pl.BlockSpec(memory_space=vmem),) * 2,
        scratch_shapes=[
            vmem((vec, rows), f32),
            vmem((ny, NX, OWN, width), bf16),
            vmem((2, 2, nz, HALF, width), bf16),
            vmem((2, ny, chunk, ncols // 2), bf16),
            vmem((ny, chunk, LANES), f32),
            vmem((vec, rows), bf16),
            vmem((lines, LANES), f32),
            vmem((NX, lines, LANES), f32),
            vmem((ny, lines, LANES), f32),
            vmem((LANES, LANES), f32),
            vmem((2, vec, ncols // 2), f32),
            vmem((vec, ncols // 2), f32),
            vmem((nz, HALF, LANES), f32),
            vmem((nz, HALF, LANES), f32),
            vmem((2, 2, nz, HALF, LANES), bf16),
            vmem((ny, NX, HALF, LANES), f32),
            vmem((ny, NX, HALF, LANES), f32),
            vmem((ny, HALF, LANES), f32),
            vmem((ny, HALF, LANES), f32),
            *sums, *sums, *sums,
            vmem((ny, NX, HALF, LANES), f32),
            dma, dma((26,)), dma((26,)), dma((ny,)), dma((ny,)), dma((ny,)),
        ],
        compiler_params=pltpu.CompilerParams(
            collective_id=0, has_side_effects=True, vmem_limit_bytes=40 << 20
        ),
        name="embed",
    )(points, start_panel.T)
    return panels.T, ritz_sum


def solution(mesh):
    in_specs = (P(("row", "col"), None), P("row", None))
    out_specs = (P("row", None), P())
    return jax.shard_map(local, mesh=mesh, in_specs=in_specs, out_specs=out_specs, check_vma=False)
```

time: 984 us -> 90.7 us (0.09)
  waiting for transfers between devices: 747 us -> 0 us
  blocking collectives: 158 us -> 0 us
  Pallas kernels: 0 us -> 86.6 us
  matrix products: 31.8 us -> 0 us
  other arithmetic: 29.8 us -> 0 us
  between operations: 14.3 us -> 0.65 us
    psum x5 -> x0, waiting for transfers between devices: 663 us -> none  [the longest x3 355 us: spread(): return lax.psum(kept, axis)]
    psum x3 -> x0, blocking collectives: 158 us -> none  [the longest x2 96.8 us: local(): lax.psum((highest(product_rows.T, product_rows), highest(panels.T, produc...]
    pallas_call x0 -> x1, Pallas kernels: none -> 86.6 us  [local(): pl.pallas_call(functools.partial(kernel, nz, ny), out_shape=(jax.ShapeDty...]
    all_gather x1 -> x0, waiting for transfers between devices: 84.6 us -> none  [local(): row_points = lax.all_gather(unit_points, 'col', axis=0, tiled=True)]
    dot_general x6 -> x0, matrix products: 27.7 us -> none  [the longest x2 11.5 us: local(): jnp.dot(affinity(row_points, col_points).astype(jnp.bfloat16), col_panel,...]
    another operation x10 -> x0, other arithmetic: 24.1 us -> none  [the longest x6 13 us: orthonormal(): factor = jnp.linalg.cholesky(gram_sum)]
  transfers between devices with their start and end apart: 6 -> 0, of which waited for: 6 -> 0; matrix products, arithmetic and copies ran while one was open for 0% -> 0% of each run, Pallas kernels for 0% -> 0%
where the time goes in v2:
time: 90.7 us; the launch traced here: 90.5 us
  Pallas kernels  86.6 us (95%)
  local copies, waits for them, and re-layouts  3.2 us (4%)
    pallas_call x1, Pallas kernels, local(): pl.pallas_call(functools.partial(kernel, nz, ny), out_shape=(jax.ShapeDty...  86.6 us
    unnamed x6, local copies, waits for them, and re-layouts  3.2 us

profile of v2, /device:TPU:1, one launch (start us, length us, event | category | flops | bytes accessed | tf_op | source)
XLA Modules:
  0.0 90.5 jit_solution(4416118458115725904)
XLA Ops:
  0.6 0.0 copy-start
  0.6 1.0 %copy-done = f32[2048,64]{0,1:T(8,128)S(1)} copy-done((f32[2048,64]{0,1:T(8,128)S(1)}, f32[2048,64]{0,1:T(8,128)}, u32[]{:S(2)}) %copy-start) | copy-done | bytes 524312
  1.7 0.0 copy-start.1
  1.7 0.8 copy-done.1
  2.4 86.6 %embed.1 = (f32[64,2048]{1,0:T(8,128)S(1)}, f32[64,64]{1,0:T(8,128)S(1)}) custom-call(f32[64,128]{1,0:T(8,128)S(1)} %copy-done.1, f32[64,2048]{1,0:T(8,128)S(1)} %bitcast.2), custom_call_target="tpu_custom_call" | custom-call | tf_op jit(solution)/shard_map/embed/pallas_call | solution.py:340
  89.1 0.8 copy.6
  89.9 0.6 copy.7
Async XLA Ops:
  0.6 1.0 %copy-start = (f32[2048,64]{0,1:T(8,128)S(1)}, f32[2048,64]{0,1:T(8,128)}, u32[]{:S(2)}) copy-start(f32[2048,64]{0,1:T(8,128)} %param.3) | copy-start | bytes 1572868
  1.7 0.8 copy-start.1

commit v3 on v2

--- a/solution.py
+++ b/solution.py
@@ -71,11 +71,10 @@
 
 def kernel(
     nz, ny, points_ref, start_ref, out_ref, ritz_ref,
-    startT, rowpts, colpts, tile, partial, scaledT, deg, deg_x, deg_y, turn,
+    pointsV, startT, rowpts, colpts, tile, partial, scaledT, deg, deg_x, deg_y, turn,
     half_c, recv_c, send_z, recv_z, scaled, send_p, recv_px, send_y, recv_py,
-    first_x, first_y, first_c, first_z, gram_x, gram_y, gram_c, gram_z,
-    ritz_x, ritz_y, ritz_c, ritz_z, whole,
-    load_sem, send_sem, recv_sem, from_y, from_x, part_x,
+    first_x, first_y, first_z, gram_x, gram_y, gram_z, ritz_x, ritz_y, ritz_z, whole,
+    load_sem, points_sem, send_sem, recv_sem, from_y, from_x, part_x,
 ):
     r, c = lax.axis_index("row"), lax.axis_index("col")
     z, core = r // 2, lax.rem(r, 2)
@@ -85,8 +84,10 @@
         "y": (ny, y, lambda p: (r, p * NX + x)),
         "z": (nz, z, lambda p: (p * 2 + core, c)),
         "c": (2, core, lambda p: (z * 2 + p, c)),
+        "xc": (2 * NX, x * 2 + core, lambda p: (z * 2 + lax.rem(p, 2), y * NX + p // 2)),
     }
-    count = (NX - 1) + (ny - 1) + (nz - 1) + 1
+    met = ("xc", "y", "z")
+    count = sum(axes[axis][0] - 1 for axis in met)
     total = nz * ny * NX * 2 * OWN
     chunk = NX * OWN
     lines = chunk // LANES
@@ -94,10 +95,14 @@
     width = points_ref.shape[1]
     vec = ritz_ref.shape[0]
 
+    load_points = pltpu.make_async_copy(points_ref, pointsV, points_sem)
+    load_points.start()
     load = pltpu.make_async_copy(start_ref, startT, load_sem)
     load.start()
     barrier = pltpu.get_barrier_semaphore()
-    for n, me, device in axes.values():
+    for axis in met:
+        n, me, device = axes[axis]
+
         def greet(i, carry):
             pl.semaphore_signal(
                 barrier, inc=1, device_id=device(lax.rem(me + i, n)), device_id_type=MESH
@@ -150,7 +155,8 @@
         return lax.rem(y + 2 * ny + (2 * lax.rem(i, 2) - 1) * ((i + 1) // 2), ny)
 
     shift = SHARPNESS * LOG2E
-    pts = points_ref[...]
+    load_points.wait()
+    pts = pointsV[...]
     unit = pts * lax.rsqrt(jnp.mean(pts * pts, axis=1, keepdims=True) + 1e-06)
     unit = (unit * math.sqrt(shift / width)).astype(bf16)
     rowpts[y, x] = unit
@@ -183,25 +189,36 @@
         tile[k, yy] = value.astype(bf16)
         return add([value[:, j:j + LANES] for j in range(0, ncols // 2, LANES)])
 
-    def near_half(i, carry):
+    def line_sums(yy, part):
+        for h in range(lines):
+            deg[pl.ds(yy * lines + h, 1), :] = jnp.sum(
+                part[h * LANES:(h + 1) * LANES].T, axis=0, keepdims=True
+            )
+
+    def chunk_here(i):
         yy = near(i)
         wait(rowpts.at[yy, pl.ds(0, NX - 1)], from_x.at[yy])
+        return yy
+
+    def near_half(i, carry):
+        yy = chunk_here(i)
         partial[yy] = affinity(yy, core)
         return carry
-    lax.fori_loop(0, ny, near_half, 0)
+
+    def far_half(i, carry):
+        yy = near(i)
+        line_sums(yy, partial[yy] + affinity(yy, 1 - core))
+        return carry
+
+    def both_halves(i, carry):
+        yy = chunk_here(i)
+        line_sums(yy, affinity(yy, core) + affinity(yy, 1 - core))
+        return carry
+    early = ny - ny // 4
+    lax.fori_loop(0, early, near_half, 0)
     arrive(3)
-
-    def far_half(i, carry):
-        for b in range(pair):
-            yy = pair * i + b
-            part = partial[yy] + affinity(yy, 1 - core)
-            for h in range(lines):
-                deg[pl.ds(yy * lines + h, 1), :] = jnp.sum(
-                    part[h * LANES:(h + 1) * LANES].T, axis=0, keepdims=True
-                )
-        return carry
-    pair = 2 if ny % 2 == 0 else 1
-    lax.fori_loop(0, ny // pair, far_half, 0)
+    lax.fori_loop(0, early, far_half, 0)
+    lax.fori_loop(early, ny, both_halves, 0)
     degrees = all_sum(4, "x", deg[...], deg_x)()
     degrees = all_sum(5, "y", degrees, deg_y)()
     inv_root = lax.rsqrt(degrees)
@@ -240,11 +257,12 @@
     send(8, "z", lambda p: scaled.at[core, :, z], scaled.at[core, :, z],
          scaled.at[0, :, pl.ds(0, nz - 1)])
     first = unpack(first_packed)
-    first_sum = all_sum(13, "c", pack(full(first, first, ((0,), (0,)))), first_c)
-    first_sum = all_sum(9, "x", first_sum(), first_x)
+    first_sum = all_sum(9, "xc", pack(full(first, first, ((0,), (0,)))), first_x)
     first_sum = all_sum(10, "y", first_sum(), first_y)
     arrive(8)
     send(11, "c", lambda p: scaled.at[core], scaled.at[core], scaled.at[0])
+
+    pair = 2 if ny % 2 == 0 else 1
 
     def product(yy, k):
         return dot(tile[k, yy], scaled[k].reshape(ncols // 2, LANES))
@@ -295,17 +313,15 @@
     second = full(unpack(second_packed), inv_first, ((1,), (1,)))
 
     whole[y, x] = pack(second)
-    gram = all_sum(16, "x", pack(full(second.T, second)), gram_x)
-    ritz = all_sum(17, "x", pack(full(basis.T, second)), ritz_x)
+    send(20, "y", lambda p: whole.at[y, x], whole.at[y, x], whole.at[pl.ds(0, ny - 1), 0])
+    gram = all_sum(16, "xc", pack(full(second, second, ((0,), (0,)))), gram_x)
+    ritz = all_sum(17, "z", pack(full(basis, second, ((0,), (0,)))), ritz_z)
     gram = all_sum(18, "y", gram(), gram_y)
-    ritz = all_sum(19, "y", ritz(), ritz_y)
-    send(20, "y", lambda p: whole.at[y, x], whole.at[y, x], whole.at[pl.ds(0, ny - 1), 0])
-    gram = all_sum(21, "c", gram(), gram_c)
-    gram = all_sum(22, "z", gram(), gram_z)
-    ritz = all_sum(23, "c", ritz(), ritz_c)
-    ritz = all_sum(24, "z", ritz(), ritz_z)
     arrive(20)
     send(25, "x", lambda p: whole.at[:, x], whole.at[:, x], whole.at[:, pl.ds(0, NX - 1)])
+    ritz = all_sum(23, "xc", ritz(), ritz_x)
+    gram = all_sum(22, "z", gram(), gram_z)
+    ritz = all_sum(19, "y", ritz(), ritz_y)
     gram = unpack(gram()) / total
     last = inverse_factor(gram)
     last = jnp.concatenate([last, jnp.zeros_like(last)], axis=1)
@@ -336,16 +352,17 @@
     ncols = 2 * nz * OWN
     vmem = pltpu.VMEM
     dma = pltpu.SemaphoreType.DMA
-    sums = [vmem((n, vec // 2, 2 * vec), f32) for n in (NX, ny, 2, nz)]
+    sums = [vmem((n, vec // 2, 2 * vec), f32) for n in (2 * NX, ny, nz)]
     panels, ritz_sum = pl.pallas_call(
         functools.partial(kernel, nz, ny),
         out_shape=(
             jax.ShapeDtypeStruct((vec, rows), f32),
             jax.ShapeDtypeStruct((vec, vec), f32),
         ),
-        in_specs=[pl.BlockSpec(memory_space=vmem), pl.BlockSpec(memory_space=pl.ANY)],
+        in_specs=[pl.BlockSpec(memory_space=pl.ANY)] * 2,
         out_specs=(pl.BlockSpec(memory_space=vmem),) * 2,
         scratch_shapes=[
+            vmem(points.shape, f32),
             vmem((vec, rows), f32),
             vmem((ny, NX, OWN, width), bf16),
             vmem((2, 2, nz, HALF, width), bf16),
@@ -367,10 +384,10 @@
             vmem((ny, HALF, LANES), f32),
             *sums, *sums, *sums,
             vmem((ny, NX, HALF, LANES), f32),
-            dma, dma((26,)), dma((26,)), dma((ny,)), dma((ny,)), dma((ny,)),
+            dma, dma, dma((26,)), dma((26,)), dma((ny,)), dma((ny,)), dma((ny,)),
         ],
         compiler_params=pltpu.CompilerParams(
-            collective_id=0, has_side_effects=True, vmem_limit_bytes=40 << 20
+            collective_id=0, has_side_effects=True, vmem_limit_bytes=60 << 20
         ),
         name="embed",
     )(points, start_panel.T)

time: 90.7 us -> 87.9 us (0.969)
  Pallas kernels: 86.6 us -> 84.6 us
    pallas_call x1, Pallas kernels: 86.6 us -> 84.6 us  [local(): pl.pallas_call(functools.partial(kernel, nz, ny), out_shape=(jax.ShapeDty...]
    unnamed x6 -> x4, local copies, waits for them, and re-layouts: 3.2 us -> 2.5 us
where the time goes in v3:
time: 87.9 us; the launch traced here: 87.7 us
  Pallas kernels  84.6 us (96%)
  local copies, waits for them, and re-layouts  2.5 us (3%)
    pallas_call x1, Pallas kernels, local(): pl.pallas_call(functools.partial(kernel, nz, ny), out_shape=(jax.ShapeDty...  84.6 us
    unnamed x4, local copies, waits for them, and re-layouts  2.5 us

profile of v3, /device:TPU:1, one launch (start us, length us, event | category | flops | bytes accessed | tf_op | source)
XLA Modules:
  0.0 87.7 jit_solution(10429961803068987156)
XLA Ops:
  0.6 84.6 %embed.1 = (f32[64,2048]{1,0:T(8,128)}, f32[64,64]{1,0:T(8,128)}) custom-call(f32[64,128]{1,0:T(8,128)} %points_ref.1, f32[64,2048]{1,0:T(8,128)} %bitcast.2), custom_call_target="tpu_custom_call" | custom-call | tf_op jit(solution)/shard_map/embed/pallas_call | solution.py:356
  85.2 0.0 copy-start
  85.2 1.9 %copy.6 = f32[2048,64]{0,1:T(8,128)} copy(f32[2048,64]{0,1:T(8,128)} %bitcast.3) | data formatting | bytes 1048576
  87.1 0.0 copy-done
  87.1 0.6 copy.7
Async XLA Ops:
  85.2 1.9 %copy-start = (f32[64,64]{1,0:T(8,128)S(1)}, f32[64,64]{1,0:T(8,128)}, u32[]{:S(2)}) copy-start(f32[64,64]{1,0:T(8,128)} %get-tuple-element.9) | copy-start | bytes 49156

commit v4 on v3

v4 whole, which is shorter than its diff:
```python
import functools
import math

import jax
import jax.numpy as jnp
from jax import lax
from jax.experimental import pallas as pl
from jax.experimental.pallas import tpu as pltpu
from jax.sharding import PartitionSpec as P

MESH = pl.DeviceIdType.MESH
NX = 4
HALF = 32
OWN = 2 * HALF
LANES = 128
SHARPNESS = 5.0
LOG2E = math.log2(math.e)
f32 = jnp.float32
bf16 = jnp.bfloat16


def dot(a, b, contract=((1,), (0,)), precision=None):
    return lax.dot_general(
        a, b, (contract, ((), ())), precision=precision, preferred_element_type=f32
    )


def full(a, b, contract=((1,), (0,))):
    return dot(a, b, contract, lax.Precision.HIGHEST)


def iota(shape, axis):
    return lax.broadcasted_iota(jnp.int32, shape, axis)


def add(parts):
    return functools.reduce(lambda a, b: a + b, parts)


def inverse_factor(gram, width=16):
    n = gram.shape[0]
    eye = jnp.where(iota((n, n), 0) == iota((n, n), 1), 1.0, 0.0).astype(f32)
    mat = jnp.concatenate([gram, eye], axis=1)
    done = []
    for b in range(0, n, width):
        m = n - b
        cols = [jnp.broadcast_to(mat[:, b + j:b + j + 1], (m, 2 * n)) for j in range(width)]
        rows = [mat[j:j + 1] for j in range(width)]
        for j in range(width):
            root = lax.rsqrt(cols[j][j:j + 1])
            cols[j], rows[j] = cols[j] * root, rows[j] * root
            for i in range(j + 1, width):
                factor = cols[j][i:i + 1]
                cols[i], rows[i] = cols[i] - factor * cols[j], rows[i] - factor * rows[j]
        done += rows
        mat = mat[width:]
        for j in range(width if m > width else 0):
            mat = mat - cols[j][width:] * rows[j]
    return jnp.concatenate(done, axis=0)[:, n:]


def pack(mat):
    n = mat.shape[0] // 2
    return jnp.concatenate([mat[:n], mat[n:]], axis=1)


def unpack(mat):
    n = mat.shape[1] // 2
    return jnp.concatenate([mat[:, :n], mat[:, n:]], axis=0)


def split(value, parts):
    out = []
    for _ in range(parts):
        out.append(value.astype(bf16))
        value = value - out[-1].astype(f32)
    return out


def kernel(
    nz, ny, points_ref, start_ref, out_ref, ritz_ref,
    points, pair_rows, pair_cols, start, rowpts, colpts, tile, colsum, deg, deg_c, deg_z, inv_col,
    panel, send_p, recv_px, send_y, recv_py, scaled, total_c, half_c, recv_c, send_z, recv_z,
    first_x, first_y, first_z, gram_x, gram_y, gram_z, ritz_x, ritz_y, ritz_z, whole, stack,
    load_sem, points_sem, send_sem, recv_sem, from_y, from_x, part_x, again_y, again_x,
):
    r, c = lax.axis_index("row"), lax.axis_index("col")
    z, core = r // 2, lax.rem(r, 2)
    y, x = c // NX, lax.rem(c, NX)
    axes = {
        "x": (NX, x, lambda p: (r, y * NX + p)),
        "y": (ny, y, lambda p: (r, p * NX + x)),
        "z": (nz, z, lambda p: (p * 2 + core, c)),
        "c": (2, core, lambda p: (z * 2 + p, c)),
        "xc": (2 * NX, x * 2 + core, lambda p: (z * 2 + lax.rem(p, 2), y * NX + p // 2)),
    }
    met = ("xc", "y", "z")
    count = sum(axes[axis][0] - 1 for axis in met)
    chunk = NX * OWN
    mid = nz * HALF
    ncols = 2 * mid
    total = 2 * ny * chunk * nz
    width = points_ref.shape[1]
    vec = ritz_ref.shape[0]

    load_points = pltpu.make_async_copy(points_ref, points, points_sem)
    load_points.start()
    here = pl.ds(pl.multiple_of(c // 2 * LANES, LANES), LANES)
    load = pltpu.make_async_copy(start_ref.at[:, here], pair_cols, load_sem)
    load.start()
    barrier = pltpu.get_barrier_semaphore()
    for axis in met:
        n, me, device = axes[axis]

        def greet(i, carry):
            pl.semaphore_signal(
                barrier, inc=1, device_id=device(lax.rem(me + i, n)), device_id_type=MESH
            )
            return carry
        lax.fori_loop(1, n, greet, 0)

    sent = {}
    pending = {}

    def send(slot, axis, src, dst, got, recv=None):
        n, me, device = axes[axis]
        arrival = recv_sem.at[slot] if recv is None else recv

        def one(i, carry):
            p = lax.rem(me + i, n)
            pltpu.make_async_remote_copy(
                src_ref=src(p), dst_ref=dst, send_sem=send_sem.at[slot],
                recv_sem=arrival, device_id=device(p), device_id_type=MESH,
            ).start()
            return carry
        lax.fori_loop(1, n, one, 0)
        sent[slot] = got
        if recv is None:
            pending[slot] = got

    def wait(ref, sem):
        pltpu.make_async_copy(ref, ref, sem).wait()

    def arrive(slot):
        wait(pending.pop(slot), recv_sem.at[slot])

    def drain():
        for slot in list(pending):
            arrive(slot)
        for slot, ref in sent.items():
            wait(ref, send_sem.at[slot])

    def all_sum(slot, axis, value, buf):
        n, me, _ = axes[axis]
        buf[me] = value
        send(slot, axis, lambda p: buf.at[me], buf.at[me], buf.at[pl.ds(0, n - 1)])

        def done():
            arrive(slot)
            return add([buf[i] for i in range(n)])
        return done

    def near(i):
        return lax.rem(y + 2 * ny + (2 * lax.rem(i, 2) - 1) * ((i + 1) // 2), ny)

    def spread(slot, buf, sems_y, sems_x):
        send(slot, "y", lambda p: buf.at[y, x], buf.at[y, x],
             buf.at[pl.ds(0, ny - 1), 0], sems_y.at[y])

        def forward(i, carry):
            yy = near(i)

            @pl.when(i > 0)
            def _():
                wait(buf.at[yy, x], sems_y.at[yy])
            send(slot + 1, "x", lambda p: buf.at[yy, x], buf.at[yy, x],
                 buf.at[:, pl.ds(0, NX - 1)], sems_x.at[yy])
            return carry

        def on():
            lax.fori_loop(0, ny, forward, 0)
            sent[slot + 1] = buf.at[:, pl.ds(0, NX - 1)]
        return on

    shift = SHARPNESS * LOG2E
    load_points.wait()
    pts = points[...]
    unit = pts * lax.rsqrt(jnp.mean(pts * pts, axis=1, keepdims=True) + 1e-06)
    unit = (unit * math.sqrt(shift / width)).astype(bf16)
    rowpts[y, x] = unit
    colpts[core, :, z] = unit.reshape(2, HALF, width)
    colsum[...] = jnp.zeros_like(colsum)

    load.wait()
    pair_rows[...] = pair_cols[...].T
    odd = lax.rem(x, 2) * OWN
    start[core, z] = jnp.concatenate(
        [pair_rows[pl.ds(odd, HALF)], pair_rows[pl.ds(odd + HALF, HALF)]], axis=1
    )

    pl.semaphore_wait(barrier, count)
    rows_on = spread(0, rowpts, from_y, from_x)
    send(2, "z", lambda p: colpts.at[core, :, z], colpts.at[core, :, z],
         colpts.at[0, :, pl.ds(0, nz - 1)])
    rows_on()
    arrive(2)
    send(3, "c", lambda p: colpts.at[core], colpts.at[core], colpts.at[0])
    send(4, "z", lambda p: start.at[core, z], start.at[core, z], start.at[0, pl.ds(0, nz - 1)])

    def affinity(yy, k):
        left = rowpts[yy].reshape(chunk, width)
        right = colpts[k].reshape(ncols, width)
        value = jnp.exp2(dot(left, right, ((1,), (1,))) - shift)
        tile[k, yy] = value.astype(bf16)
        colsum[k] = colsum[k] + jnp.sum(value.reshape(chunk // 8, 8, ncols), axis=0)

    def chunk_here(i):
        yy = near(i)
        wait(rowpts.at[yy, pl.ds(0, NX - 1)], from_x.at[yy])
        return yy

    def near_half(i, carry):
        affinity(chunk_here(i), core)
        return carry

    def far_half(i, carry):
        affinity(near(i), 1 - core)
        return carry

    def both_halves(i, carry):
        yy = chunk_here(i)
        affinity(yy, core)
        affinity(yy, 1 - core)
        return carry
    early = ny - ny // 4
    lax.fori_loop(0, early, near_half, 0)
    arrive(3)
    lax.fori_loop(0, early, far_half, 0)
    lax.fori_loop(early, ny, both_halves, 0)
    lines = ncols // LANES
    for k in range(2):
        line = jnp.sum(colsum[k], axis=0, keepdims=True)
        for j in range(lines):
            deg[k * lines + j:k * lines + j + 1] = line[:, j * LANES:(j + 1) * LANES]

    degrees = all_sum(5, "c", deg[...], deg_c)
    arrive(4)
    send(6, "c", lambda p: start.at[core], start.at[core], start.at[0])
    degrees = all_sum(7, "z", degrees(), deg_z)
    arrive(6)
    inv_root = lax.rsqrt(degrees())
    for k in range(2):
        for j in range(lines):
            row = inv_root[k * lines + j:k * lines + j + 1]
            inv_col[k, j * LANES:(j + 1) * LANES] = jnp.broadcast_to(row, (LANES, LANES)).T
    low = iota((mid, LANES), 1) < vec
    for k in range(2):
        one = start[k].reshape(mid, LANES)
        two = pltpu.roll(one, vec, 1)
        panel[k, :mid] = (jnp.where(low, one, two) * inv_col[k, :mid]).astype(bf16)
        panel[k, mid:] = (jnp.where(low, two, one) * inv_col[k, mid:]).astype(bf16)
    keep = iota((HALF, LANES), 1) < vec
    inv_packed = jnp.where(
        keep, inv_col[core, pl.ds(z * HALF, HALF)], inv_col[core, pl.ds(mid + z * HALF, HALF)]
    )

    def product(j, carry):
        yy = near(ny - 1 - j)
        out = dot(tile[0, yy], panel[0]) + dot(tile[1, yy], panel[1])
        for s in range(NX):
            send_p[yy, s] = jnp.where(
                keep, out[s * OWN:s * OWN + HALF], out[s * OWN + HALF:(s + 1) * OWN]
            ).astype(bf16)
        send(8, "x", lambda p: send_p.at[yy, p], recv_px.at[yy, x],
             send_p.at[:, pl.ds(0, NX - 1)], part_x.at[yy])
        recv_px[yy, x] = send_p[yy, x]
        return carry
    lax.fori_loop(0, ny, product, 0)
    sent[8] = send_p.at[:, pl.ds(0, NX - 1)]

    def collect(j, carry):
        yy = near(ny - 1 - j)
        wait(recv_px.at[yy, pl.ds(0, NX - 1)], part_x.at[yy])
        send_y[yy] = add([recv_px[yy, i].astype(f32) for i in range(NX)])

        @pl.when(j < ny - 1)
        def _():
            pltpu.make_async_remote_copy(
                src_ref=send_y.at[yy], dst_ref=recv_py.at[y], send_sem=send_sem.at[9],
                recv_sem=recv_sem.at[9], device_id=(r, yy * NX + x), device_id_type=MESH,
            ).start()
        return carry
    lax.fori_loop(0, ny, collect, 0)
    sent[9] = pending[9] = recv_py.at[pl.ds(0, ny - 1)]
    recv_py[y] = send_y[y]
    arrive(9)
    first_packed = add([recv_py[i] for i in range(ny)]) * inv_packed

    scaled[y, x] = jnp.concatenate(split(unpack(first_packed * inv_packed), 2), axis=1)
    scaled_on = spread(10, scaled, again_y, again_x)
    first = unpack(first_packed)
    first_sum = all_sum(12, "z", pack(full(first, first, ((0,), (0,)))), first_z)
    scaled_on()
    first_sum = all_sum(13, "xc", first_sum(), first_x)

    def transposed(i, k):
        yy = near(i)
        left = scaled[yy].reshape(chunk, 2 * vec).T
        return dot(left, tile[k, yy])

    def chunk_there(i):
        yy = near(i)
        wait(scaled.at[yy, pl.ds(0, NX - 1)], again_x.at[yy])

    def gather(i, carry):
        chunk_there(i)
        for k in range(2):
            total_c[k] = total_c[k] + transposed(i, k)
        return carry
    chunk_there(0)
    for k in range(2):
        total_c[k] = transposed(0, k)
    lax.fori_loop(1, ny, gather, 0)
    for k in range(2):
        half_c[k] = total_c[k, :vec] + total_c[k, vec:]
    send(14, "c", lambda p: half_c.at[p], recv_c, recv_c)
    first_sum = all_sum(15, "y", first_sum(), first_y)
    arrive(14)
    both = half_c[core] + recv_c[...]
    both = jnp.concatenate([both[:, :mid], both[:, mid:]], axis=0).T
    send_z[...] = both.reshape(send_z.shape)
    send(16, "z", lambda p: send_z.at[p], recv_z.at[z], recv_z.at[pl.ds(0, nz - 1)])
    recv_z[z] = send_z[z]
    inv_first = inverse_factor(unpack(first_sum()) / total)
    basis = full(first, inv_first, ((1,), (1,)))
    arrive(16)
    second_packed = add([recv_z[i] for i in range(nz)]) * inv_packed
    second = full(unpack(second_packed), inv_first, ((1,), (1,)))

    whole[y, x] = pack(second)
    send(20, "y", lambda p: whole.at[y, x], whole.at[y, x], whole.at[pl.ds(0, ny - 1), 0])
    gram = all_sum(17, "xc", pack(full(second, second, ((0,), (0,)))), gram_x)
    ritz = all_sum(18, "z", pack(full(basis, second, ((0,), (0,)))), ritz_z)
    gram = all_sum(19, "y", gram(), gram_y)
    arrive(20)
    send(21, "x", lambda p: whole.at[:, x], whole.at[:, x], whole.at[:, pl.ds(0, NX - 1)])
    ritz = all_sum(22, "xc", ritz(), ritz_x)
    gram = all_sum(23, "z", gram(), gram_z)
    ritz = all_sum(24, "y", ritz(), ritz_y)
    arrive(21)

    def prepare(yy, carry):
        parts = []
        for s in range(NX):
            block = whole[yy, s]
            parts += [block, pltpu.roll(block, vec, 1)]
        high, middle, low = split(jnp.concatenate(parts, axis=0).T[:vec], 3)
        columns = pl.ds(pl.multiple_of(yy * chunk, chunk), chunk)
        stack[:, columns] = jnp.concatenate([high, middle, low, high, middle, high], axis=0)
        return carry
    lax.fori_loop(0, ny, prepare, 0)
    last = inverse_factor(unpack(gram()) / total)
    high, middle, low = [part.astype(f32) for part in split(last, 3)]
    last = jnp.concatenate([high, high, high, middle, middle, low], axis=1).astype(bf16)
    block = min(4 * chunk, ny * chunk)
    for j in range(0, ny * chunk, block):
        out_ref[:, j:j + block] = dot(last, stack[:, j:j + block])
    ritz_ref[...] = unpack(ritz()) / total
    drain()


def hand_over(panels_ref, ritz_ref, panels_out, ritz_out, sems):
    copies = [
        pltpu.make_async_copy(panels_ref, panels_out, sems.at[0]),
        pltpu.make_async_copy(ritz_ref, ritz_out, sems.at[1]),
    ]
    for copy in copies:
        copy.start()
    for copy in copies:
        copy.wait()


def local(points, start_panel):
    nz = lax.axis_size("row") // 2
    ny = lax.axis_size("col") // NX
    rows, vec = start_panel.shape
    width = points.shape[1]
    chunk = NX * OWN
    mid = nz * HALF
    ncols = 2 * mid
    lines = 2 * ncols // LANES
    vmem = pltpu.VMEM
    dma = pltpu.SemaphoreType.DMA
    anywhere = pl.BlockSpec(memory_space=pl.ANY)
    sums = [vmem((n, vec // 2, 2 * vec), f32) for n in (2 * NX, ny, nz)]
    out_shape = (
        jax.ShapeDtypeStruct((vec, rows), f32),
        jax.ShapeDtypeStruct((vec, vec), f32),
    )
    results = pl.pallas_call(
        functools.partial(kernel, nz, ny),
        out_shape=out_shape,
        in_specs=[anywhere] * 2,
        out_specs=(pl.BlockSpec(memory_space=vmem),) * 2,
        scratch_shapes=[
            vmem(points.shape, f32),
            vmem((LANES, vec), f32),
            vmem((vec, LANES), f32),
            vmem((2, nz, HALF, LANES), f32),
            vmem((ny, NX, OWN, width), bf16),
            vmem((2, 2, nz, HALF, width), bf16),
            vmem((2, ny, chunk, ncols), bf16),
            vmem((2, 8, ncols), f32),
            vmem((lines, LANES), f32),
            vmem((2, lines, LANES), f32),
            vmem((nz, lines, LANES), f32),
            vmem((2, ncols, LANES), f32),
            vmem((2, ncols, LANES), bf16),
            vmem((ny, NX, HALF, LANES), bf16),
            vmem((ny, NX, HALF, LANES), bf16),
            vmem((ny, HALF, LANES), f32),
            vmem((ny, HALF, LANES), f32),
            vmem((ny, NX, OWN, LANES), bf16),
            vmem((2, LANES, ncols), f32),
            vmem((2, vec, ncols), f32),
            vmem((vec, ncols), f32),
            vmem((nz, HALF, LANES), f32),
            vmem((nz, HALF, LANES), f32),
            *sums, *sums, *sums,
            vmem((ny, NX, HALF, LANES), f32),
            vmem((6 * vec, rows), bf16),
            dma, dma, dma((25,)), dma((25,)), dma((ny,)), dma((ny,)), dma((ny,)), dma((ny,)), dma((ny,)),
        ],
        compiler_params=pltpu.CompilerParams(
            collective_id=0, has_side_effects=True, vmem_limit_bytes=60 << 20
        ),
        name="embed",
    )(points, start_panel.T)
    panels, ritz_sum = pl.pallas_call(
        hand_over,
        out_shape=out_shape,
        in_specs=[anywhere] * 2,
        out_specs=(anywhere,) * 2,
        scratch_shapes=[dma((2,))],
        compiler_params=pltpu.CompilerParams(vmem_limit_bytes=60 << 20),
        name="hand_over",
    )(*results)
    return panels.T, ritz_sum


def solution(mesh):
    in_specs = (P(("row", "col"), None), P("row", None))
    out_specs = (P("row", None), P())
    return jax.shard_map(local, mesh=mesh, in_specs=in_specs, out_specs=out_specs, check_vma=False)
```

time: 87.9 us -> 102 us (1.16)
  Pallas kernels: 84.6 us -> 102 us
  local copies, waits for them, and re-layouts: 2.5 us -> 0 us
    pallas_call x1 -> x2, Pallas kernels: 84.6 us -> 102 us  [the longest x1 83.5 us: local(): pl.pallas_call(functools.partial(kernel, nz, ny), out_shape=out_shape, in...]
    unnamed x4 -> x0, local copies, waits for them, and re-layouts: 2.5 us -> none
where the time goes in v4:
time: 102 us
  Pallas kernels  102 us (100%)
    pallas_call x1, Pallas kernels, local(): pl.pallas_call(functools.partial(kernel, nz, ny), out_shape=out_shape, in...  83.5 us
    pallas_call x1, Pallas kernels, local(): pl.pallas_call(hand_over, out_shape=out_shape, in_specs=[anywhere] * 2, o...  18 us

profile of v4, /device:TPU:1, one launch (start us, length us, event | category | flops | bytes accessed | tf_op | source)
XLA Modules:
  0.0 102.1 jit_solution(4352079213454516646)
XLA Ops:
  0.6 83.5 %embed.1 = (f32[64,2048]{1,0:T(8,128)}, f32[64,64]{1,0:T(8,128)}) custom-call(f32[64,128]{1,0:T(8,128)} %points_ref.1, f32[64,2048]{1,0:T(8,128)} %bitcast.2), custom_call_target="tpu_custom_call" | custom-call | tf_op jit(solution)/shard_map/embed/pallas_call | solution.py:400
  84.2 18.0 %hand_over.1 = (f32[64,2048]{1,0:T(8,128)}, f32[64,64]{1,0:T(8,128)}) custom-call(f32[64,2048]{1,0:T(8,128)} %get-tuple-element.6.panels_ref, f32[64,64]{1,0:T(8,128)} %get-tuple-element.7.ritz_ref), custom_call_target="tpu_custom_call" | custom-call | tf_op jit(solution)/shard_map/hand_over/pallas_call | solution.py:439

commit v5 on v4

--- a/solution.py
+++ b/solution.py
@@ -281,7 +281,7 @@
     def collect(j, carry):
         yy = near(ny - 1 - j)
         wait(recv_px.at[yy, pl.ds(0, NX - 1)], part_x.at[yy])
-        send_y[yy] = add([recv_px[yy, i].astype(f32) for i in range(NX)])
+        send_y[yy] = add([recv_px[yy, i].astype(f32) for i in range(NX)]).astype(bf16)
 
         @pl.when(j < ny - 1)
         def _():
@@ -294,7 +294,7 @@
     sent[9] = pending[9] = recv_py.at[pl.ds(0, ny - 1)]
     recv_py[y] = send_y[y]
     arrive(9)
-    first_packed = add([recv_py[i] for i in range(ny)]) * inv_packed
+    first_packed = add([recv_py[i].astype(f32) for i in range(ny)]) * inv_packed
 
     scaled[y, x] = jnp.concatenate(split(unpack(first_packed * inv_packed), 2), axis=1)
     scaled_on = spread(10, scaled, again_y, again_x)
@@ -320,11 +320,13 @@
     chunk_there(0)
     for k in range(2):
         total_c[k] = transposed(0, k)
-    lax.fori_loop(1, ny, gather, 0)
+    late = max(ny - 2, 1)
+    lax.fori_loop(1, late, gather, 0)
+    first_sum = all_sum(15, "y", first_sum(), first_y)
+    lax.fori_loop(late, ny, gather, 0)
     for k in range(2):
         half_c[k] = total_c[k, :vec] + total_c[k, vec:]
     send(14, "c", lambda p: half_c.at[p], recv_c, recv_c)
-    first_sum = all_sum(15, "y", first_sum(), first_y)
     arrive(14)
     both = half_c[core] + recv_c[...]
     both = jnp.concatenate([both[:, :mid], both[:, mid:]], axis=0).T
@@ -332,19 +334,28 @@
     send(16, "z", lambda p: send_z.at[p], recv_z.at[z], recv_z.at[pl.ds(0, nz - 1)])
     recv_z[z] = send_z[z]
     inv_first = inverse_factor(unpack(first_sum()) / total)
-    basis = full(first, inv_first, ((1,), (1,)))
+    none = jnp.zeros_like(inv_first)
+    twice = jnp.concatenate(
+        [jnp.concatenate([inv_first, none], axis=1), jnp.concatenate([none, inv_first], axis=1)],
+        axis=0,
+    )
+    basis_packed = full(first_packed, twice, ((1,), (1,)))
+
+    def product_sums(left, right):
+        both = full(left, right, ((0,), (0,)))
+        return pack(both[:vec, :vec] + both[vec:, vec:])
     arrive(16)
     second_packed = add([recv_z[i] for i in range(nz)]) * inv_packed
-    second = full(unpack(second_packed), inv_first, ((1,), (1,)))
-
-    whole[y, x] = pack(second)
+    second_packed = full(second_packed, twice, ((1,), (1,)))
+
+    whole[y, x] = second_packed
     send(20, "y", lambda p: whole.at[y, x], whole.at[y, x], whole.at[pl.ds(0, ny - 1), 0])
-    gram = all_sum(17, "xc", pack(full(second, second, ((0,), (0,)))), gram_x)
-    ritz = all_sum(18, "z", pack(full(basis, second, ((0,), (0,)))), ritz_z)
+    gram = all_sum(17, "xc", product_sums(second_packed, second_packed), gram_x)
+    ritz = all_sum(18, "z", product_sums(basis_packed, second_packed), ritz_z)
     gram = all_sum(19, "y", gram(), gram_y)
+    ritz = all_sum(22, "xc", ritz(), ritz_x)
     arrive(20)
     send(21, "x", lambda p: whole.at[:, x], whole.at[:, x], whole.at[:, pl.ds(0, NX - 1)])
-    ritz = all_sum(22, "xc", ritz(), ritz_x)
     gram = all_sum(23, "z", gram(), gram_z)
     ritz = all_sum(24, "y", ritz(), ritz_y)
     arrive(21)
@@ -391,7 +402,7 @@
     lines = 2 * ncols // LANES
     vmem = pltpu.VMEM
     dma = pltpu.SemaphoreType.DMA
-    anywhere = pl.BlockSpec(memory_space=pl.ANY)
+    hbm = pl.BlockSpec(memory_space=pltpu.HBM)
     sums = [vmem((n, vec // 2, 2 * vec), f32) for n in (2 * NX, ny, nz)]
     out_shape = (
         jax.ShapeDtypeStruct((vec, rows), f32),
@@ -400,7 +411,7 @@
     results = pl.pallas_call(
         functools.partial(kernel, nz, ny),
         out_shape=out_shape,
-        in_specs=[anywhere] * 2,
+        in_specs=[hbm] * 2,
         out_specs=(pl.BlockSpec(memory_space=vmem),) * 2,
         scratch_shapes=[
             vmem(points.shape, f32),
@@ -418,8 +429,8 @@
             vmem((2, ncols, LANES), bf16),
             vmem((ny, NX, HALF, LANES), bf16),
             vmem((ny, NX, HALF, LANES), bf16),
-            vmem((ny, HALF, LANES), f32),
-            vmem((ny, HALF, LANES), f32),
+            vmem((ny, HALF, LANES), bf16),
+            vmem((ny, HALF, LANES), bf16),
             vmem((ny, NX, OWN, LANES), bf16),
             vmem((2, LANES, ncols), f32),
             vmem((2, vec, ncols), f32),
@@ -432,17 +443,17 @@
             dma, dma, dma((25,)), dma((25,)), dma((ny,)), dma((ny,)), dma((ny,)), dma((ny,)), dma((ny,)),
         ],
         compiler_params=pltpu.CompilerParams(
-            collective_id=0, has_side_effects=True, vmem_limit_bytes=60 << 20
+            collective_id=0, has_side_effects=True, vmem_limit_bytes=53 << 20
         ),
         name="embed",
     )(points, start_panel.T)
     panels, ritz_sum = pl.pallas_call(
         hand_over,
         out_shape=out_shape,
-        in_specs=[anywhere] * 2,
-        out_specs=(anywhere,) * 2,
+        in_specs=[pl.BlockSpec(memory_space=pl.ANY)] * 2,
+        out_specs=(hbm,) * 2,
         scratch_shapes=[dma((2,))],
-        compiler_params=pltpu.CompilerParams(vmem_limit_bytes=60 << 20),
+        compiler_params=pltpu.CompilerParams(vmem_limit_bytes=4 << 20),
         name="hand_over",
     )(*results)
     return panels.T, ritz_sum

time: 102 us -> 82.7 us (0.81)
  Pallas kernels: 102 us -> 80.4 us
    pallas_call x1, Pallas kernels: 18 us -> 0.81 us  [local(): pl.pallas_call(hand_over, out_shape=out_shape, in_specs=[pl.BlockSpec(mem...]
    pallas_call x1, Pallas kernels: 83.5 us -> 79.6 us  [local(): pl.pallas_call(functools.partial(kernel, nz, ny), out_shape=out_shape, in...]
where the time goes in v5:
time: 82.7 us; the launch traced here: 81.8 us
  Pallas kernels  80.4 us (97%)
    pallas_call x1, Pallas kernels, local(): pl.pallas_call(functools.partial(kernel, nz, ny), out_shape=out_shape, in...  79.6 us

profile of v5, /device:TPU:1, one launch (start us, length us, event | category | flops | bytes accessed | tf_op | source)
XLA Modules:
  0.0 81.8 jit_solution(1702844031422802889)
XLA Ops:
  0.6 0.0 copy-start
  0.6 0.7 copy-done
  1.4 79.6 %embed.1 = (f32[64,2048]{1,0:T(8,128)S(1)}, f32[64,64]{1,0:T(8,128)S(1)}) custom-call(f32[64,128]{1,0:T(8,128)S(1)} %copy-done, f32[64,2048]{1,0:T(8,128)} %bitcast.2), custom_call_target="tpu_custom_call" | custom-call | tf_op jit(solution)/shard_map/embed/pallas_call | solution.py:411
  81.0 0.8 hand_over.1
Async XLA Ops:
  0.6 0.8 copy-start

commit v6 on v5

--- a/solution.py
+++ b/solution.py
@@ -79,7 +79,7 @@
 
 def kernel(
     nz, ny, points_ref, start_ref, out_ref, ritz_ref,
-    points, pair_rows, pair_cols, start, rowpts, colpts, tile, colsum, deg, deg_c, deg_z, inv_col,
+    points, pair_rows, pair_cols, start, rowpts, colpts, tile, colsum, deg, deg_zc, inv_col,
     panel, send_p, recv_px, send_y, recv_py, scaled, total_c, half_c, recv_c, send_z, recv_z,
     first_x, first_y, first_z, gram_x, gram_y, gram_z, ritz_x, ritz_y, ritz_z, whole, stack,
     load_sem, points_sem, send_sem, recv_sem, from_y, from_x, part_x, again_y, again_x,
@@ -94,7 +94,12 @@
         "c": (2, core, lambda p: (z * 2 + p, c)),
         "xc": (2 * NX, x * 2 + core, lambda p: (z * 2 + lax.rem(p, 2), y * NX + p // 2)),
     }
-    met = ("xc", "y", "z")
+    axes["zc"] = (2 * nz, r, lambda p: (p, c))
+    axes["other core"] = (nz, z, lambda p: (p * 2 + 1 - core, c))
+    beside = [lax.rem(y + step, ny) for step in ((1, ny - 1) if ny > 2 else range(1, ny))]
+    for i, yy in enumerate(beside):
+        axes[i] = (NX, x, lambda p, yy=yy: (r, yy * NX + p))
+    met = ["xc", "y", "z", "other core", *range(len(beside))]
     count = sum(axes[axis][0] - 1 for axis in met)
     chunk = NX * OWN
     mid = nz * HALF
@@ -166,19 +171,21 @@
     def spread(slot, buf, sems_y, sems_x):
         send(slot, "y", lambda p: buf.at[y, x], buf.at[y, x],
              buf.at[pl.ds(0, ny - 1), 0], sems_y.at[y])
+        for axis in ("x", *range(len(beside))):
+            send(slot + 1, axis, lambda p: buf.at[y, x], buf.at[y, x],
+                 buf.at[:, pl.ds(0, NX - 1)], sems_x.at[y])
 
         def forward(i, carry):
             yy = near(i)
-
-            @pl.when(i > 0)
-            def _():
-                wait(buf.at[yy, x], sems_y.at[yy])
+            wait(buf.at[yy, x], sems_y.at[yy])
             send(slot + 1, "x", lambda p: buf.at[yy, x], buf.at[yy, x],
                  buf.at[:, pl.ds(0, NX - 1)], sems_x.at[yy])
             return carry
 
         def on():
-            lax.fori_loop(0, ny, forward, 0)
+            lax.fori_loop(1 + len(beside), ny, forward, 0)
+            for yy in beside:
+                wait(buf.at[yy, x], sems_y.at[yy])
             sent[slot + 1] = buf.at[:, pl.ds(0, NX - 1)]
         return on
 
@@ -243,10 +250,9 @@
         for j in range(lines):
             deg[k * lines + j:k * lines + j + 1] = line[:, j * LANES:(j + 1) * LANES]
 
-    degrees = all_sum(5, "c", deg[...], deg_c)
+    degrees = all_sum(5, "zc", deg[...], deg_zc)
     arrive(4)
     send(6, "c", lambda p: start.at[core], start.at[core], start.at[0])
-    degrees = all_sum(7, "z", degrees(), deg_z)
     arrive(6)
     inv_root = lax.rsqrt(degrees())
     for k in range(2):
@@ -264,18 +270,29 @@
         keep, inv_col[core, pl.ds(z * HALF, HALF)], inv_col[core, pl.ds(mid + z * HALF, HALF)]
     )
 
-    def product(j, carry):
+    pair = 2 if ny % 2 == 0 else 1
+
+    def product(j):
         yy = near(ny - 1 - j)
         out = dot(tile[0, yy], panel[0]) + dot(tile[1, yy], panel[1])
         for s in range(NX):
             send_p[yy, s] = jnp.where(
                 keep, out[s * OWN:s * OWN + HALF], out[s * OWN + HALF:(s + 1) * OWN]
             ).astype(bf16)
+
+    def hand_on(j):
+        yy = near(ny - 1 - j)
         send(8, "x", lambda p: send_p.at[yy, p], recv_px.at[yy, x],
              send_p.at[:, pl.ds(0, NX - 1)], part_x.at[yy])
         recv_px[yy, x] = send_p[yy, x]
-        return carry
-    lax.fori_loop(0, ny, product, 0)
+
+    def products(j, carry):
+        for b in range(pair):
+            product(pair * j + b)
+        for b in range(pair):
+            hand_on(pair * j + b)
+        return carry
+    lax.fori_loop(0, ny // pair, products, 0)
     sent[8] = send_p.at[:, pl.ds(0, NX - 1)]
 
     def collect(j, carry):
@@ -301,7 +318,7 @@
     first = unpack(first_packed)
     first_sum = all_sum(12, "z", pack(full(first, first, ((0,), (0,)))), first_z)
     scaled_on()
-    first_sum = all_sum(13, "xc", first_sum(), first_x)
+    first_sum = all_sum(15, "y", first_sum(), first_y)
 
     def transposed(i, k):
         yy = near(i)
@@ -320,13 +337,11 @@
     chunk_there(0)
     for k in range(2):
         total_c[k] = transposed(0, k)
-    late = max(ny - 2, 1)
-    lax.fori_loop(1, late, gather, 0)
-    first_sum = all_sum(15, "y", first_sum(), first_y)
-    lax.fori_loop(late, ny, gather, 0)
+    lax.fori_loop(1, ny, gather, 0)
     for k in range(2):
         half_c[k] = total_c[k, :vec] + total_c[k, vec:]
     send(14, "c", lambda p: half_c.at[p], recv_c, recv_c)
+    first_sum = all_sum(13, "xc", first_sum(), first_x)
     arrive(14)
     both = half_c[core] + recv_c[...]
     both = jnp.concatenate([both[:, :mid], both[:, mid:]], axis=0).T
@@ -423,8 +438,7 @@
             vmem((2, ny, chunk, ncols), bf16),
             vmem((2, 8, ncols), f32),
             vmem((lines, LANES), f32),
-            vmem((2, lines, LANES), f32),
-            vmem((nz, lines, LANES), f32),
+            vmem((2 * nz, lines, LANES), f32),
             vmem((2, ncols, LANES), f32),
             vmem((2, ncols, LANES), bf16),
             vmem((ny, NX, HALF, LANES), bf16),

time: 82.7 us -> 80.5 us (0.973)
  Pallas kernels: 80.4 us -> 78.8 us
    pallas_call x1, Pallas kernels: 79.6 us -> 78 us  [local(): pl.pallas_call(functools.partial(kernel, nz, ny), out_shape=out_shape, in...]
where the time goes in v6:
time: 80.5 us; the launch traced here: 80.2 us
  Pallas kernels  78.8 us (98%)
    pallas_call x1, Pallas kernels, local(): pl.pallas_call(functools.partial(kernel, nz, ny), out_shape=out_shape, in...  78 us

profile of v6, /device:TPU:1, one launch (start us, length us, event | category | flops | bytes accessed | tf_op | source)
XLA Modules:
  0.0 80.2 jit_solution(10899060562148841890)
XLA Ops:
  0.6 0.0 copy-start
  0.6 0.7 copy-done
  1.4 78.0 %embed.1 = (f32[64,2048]{1,0:T(8,128)S(1)}, f32[64,64]{1,0:T(8,128)S(1)}) custom-call(f32[64,128]{1,0:T(8,128)S(1)} %copy-done, f32[64,2048]{1,0:T(8,128)} %bitcast.2), custom_call_target="tpu_custom_call" | custom-call | tf_op jit(solution)/shard_map/embed/pallas_call | solution.py:426
  79.4 0.8 %hand_over.1 = (f32[64,2048]{1,0:T(8,128)}, f32[64,64]{1,0:T(8,128)}) custom-call(f32[64,2048]{1,0:T(8,128)S(1)} %get-tuple-element.6.panels_ref, f32[64,64]{1,0:T(8,128)S(1)} %get-tuple-element.7.ritz_ref), custom_call_target="tpu_custom_call" | custom-call | tf_op jit(solution)/shard_map/hand_over/pallas_call | solution.py:464
Async XLA Ops:
  0.6 0.8 copy-start

commit v7 on v6

--- a/solution.py
+++ b/solution.py
@@ -75,6 +75,10 @@
         out.append(value.astype(bf16))
         value = value - out[-1].astype(f32)
     return out
+
+
+def far(i, me, n):
+    return lax.rem(me + n // 2 + (1 - 2 * lax.rem(i, 2)) * ((i + 1) // 2), n)
 
 
 def kernel(
@@ -119,10 +123,10 @@
 
         def greet(i, carry):
             pl.semaphore_signal(
-                barrier, inc=1, device_id=device(lax.rem(me + i, n)), device_id_type=MESH
+                barrier, inc=1, device_id=device(far(i, me, n)), device_id_type=MESH
             )
             return carry
-        lax.fori_loop(1, n, greet, 0)
+        lax.fori_loop(0, n - 1, greet, 0)
 
     sent = {}
     pending = {}
@@ -132,13 +136,13 @@
         arrival = recv_sem.at[slot] if recv is None else recv
 
         def one(i, carry):
-            p = lax.rem(me + i, n)
+            p = far(i, me, n)
             pltpu.make_async_remote_copy(
                 src_ref=src(p), dst_ref=dst, send_sem=send_sem.at[slot],
                 recv_sem=arrival, device_id=device(p), device_id_type=MESH,
             ).start()
             return carry
-        lax.fori_loop(1, n, one, 0)
+        lax.fori_loop(0, n - 1, one, 0)
         sent[slot] = got
         if recv is None:
             pending[slot] = got

time: 80.5 us -> 80 us (level)
  no operation moved by 1% of the time
where the time goes in v7:
time: 80 us; the launch traced here: 79.8 us
  Pallas kernels  78.4 us (98%)
    pallas_call x1, Pallas kernels, local(): pl.pallas_call(functools.partial(kernel, nz, ny), out_shape=out_shape, in...  77.6 us

profile of v7, /device:TPU:1, one launch (start us, length us, event | category | flops | bytes accessed | tf_op | source)
XLA Modules:
  0.0 79.8 jit_solution(8192616809577392868)
XLA Ops:
  0.6 0.0 copy-start
  0.6 0.7 copy-done
  1.4 77.6 %embed.1 = (f32[64,2048]{1,0:T(8,128)S(1)}, f32[64,64]{1,0:T(8,128)S(1)}) custom-call(f32[64,128]{1,0:T(8,128)S(1)} %copy-done, f32[64,2048]{1,0:T(8,128)} %bitcast.2), custom_call_target="tpu_custom_call" | custom-call | tf_op jit(solution)/shard_map/embed/pallas_call | solution.py:430
  79.0 0.8 %hand_over.1 = (f32[64,2048]{1,0:T(8,128)}, f32[64,64]{1,0:T(8,128)}) custom-call(f32[64,2048]{1,0:T(8,128)S(1)} %get-tuple-element.6.panels_ref, f32[64,64]{1,0:T(8,128)S(1)} %get-tuple-element.7.ritz_ref), custom_call_target="tpu_custom_call" | custom-call | tf_op jit(solution)/shard_map/hand_over/pallas_call | solution.py:468
Async XLA Ops:
  0.6 0.8 copy-start

commit v8 on v7

--- a/solution.py
+++ b/solution.py
@@ -84,7 +84,7 @@
 def kernel(
     nz, ny, points_ref, start_ref, out_ref, ritz_ref,
     points, pair_rows, pair_cols, start, rowpts, colpts, tile, colsum, deg, deg_zc, inv_col,
-    panel, send_p, recv_px, send_y, recv_py, scaled, total_c, half_c, recv_c, send_z, recv_z,
+    laid_out, panel, send_p, recv_px, send_y, recv_py, scaled, total_c, half_c, recv_c, send_z, recv_z,
     first_x, first_y, first_z, gram_x, gram_y, gram_z, ritz_x, ritz_y, ritz_z, whole, stack,
     load_sem, points_sem, send_sem, recv_sem, from_y, from_x, part_x, again_y, again_x,
 ):
@@ -258,17 +258,20 @@
     arrive(4)
     send(6, "c", lambda p: start.at[core], start.at[core], start.at[0])
     arrive(6)
+    low = iota((mid, LANES), 1) < vec
+    for k in range(2):
+        one = start[k].reshape(mid, LANES)
+        two = pltpu.roll(one, vec, 1)
+        laid_out[k, :mid] = jnp.where(low, one, two)
+        laid_out[k, mid:] = jnp.where(low, two, one)
     inv_root = lax.rsqrt(degrees())
     for k in range(2):
         for j in range(lines):
             row = inv_root[k * lines + j:k * lines + j + 1]
-            inv_col[k, j * LANES:(j + 1) * LANES] = jnp.broadcast_to(row, (LANES, LANES)).T
-    low = iota((mid, LANES), 1) < vec
-    for k in range(2):
-        one = start[k].reshape(mid, LANES)
-        two = pltpu.roll(one, vec, 1)
-        panel[k, :mid] = (jnp.where(low, one, two) * inv_col[k, :mid]).astype(bf16)
-        panel[k, mid:] = (jnp.where(low, two, one) * inv_col[k, mid:]).astype(bf16)
+            inv = jnp.broadcast_to(row, (LANES, LANES)).T
+            part = slice(j * LANES, (j + 1) * LANES)
+            inv_col[k, part] = inv
+            panel[k, part] = (laid_out[k, part] * inv).astype(bf16)
     keep = iota((HALF, LANES), 1) < vec
     inv_packed = jnp.where(
         keep, inv_col[core, pl.ds(z * HALF, HALF)], inv_col[core, pl.ds(mid + z * HALF, HALF)]
@@ -341,10 +344,16 @@
     chunk_there(0)
     for k in range(2):
         total_c[k] = transposed(0, k)
-    lax.fori_loop(1, ny, gather, 0)
-    for k in range(2):
-        half_c[k] = total_c[k, :vec] + total_c[k, vec:]
+    lax.fori_loop(1, ny - 1, gather, 0)
+
+    def last_chunk(k):
+        both = total_c[k] + transposed(ny - 1, k) if ny > 1 else total_c[k]
+        half_c[k] = both[:vec] + both[vec:]
+    if ny > 1:
+        chunk_there(ny - 1)
+    last_chunk(1 - core)
     send(14, "c", lambda p: half_c.at[p], recv_c, recv_c)
+    last_chunk(core)
     first_sum = all_sum(13, "xc", first_sum(), first_x)
     arrive(14)
     both = half_c[core] + recv_c[...]
@@ -400,10 +409,11 @@
 
 
 def hand_over(panels_ref, ritz_ref, panels_out, ritz_out, sems):
-    copies = [
-        pltpu.make_async_copy(panels_ref, panels_out, sems.at[0]),
-        pltpu.make_async_copy(ritz_ref, ritz_out, sems.at[1]),
-    ]
+    step = panels_ref.shape[0] // 4
+    copies = [pltpu.make_async_copy(ritz_ref, ritz_out, sems.at[4])]
+    for i in range(4):
+        part = pl.ds(i * step, step)
+        copies.append(pltpu.make_async_copy(panels_ref.at[part], panels_out.at[part], sems.at[i]))
     for copy in copies:
         copy.start()
     for copy in copies:
@@ -444,6 +454,7 @@
             vmem((lines, LANES), f32),
             vmem((2 * nz, lines, LANES), f32),
             vmem((2, ncols, LANES), f32),
+            vmem((2, ncols, LANES), f32),
             vmem((2, ncols, LANES), bf16),
             vmem((ny, NX, HALF, LANES), bf16),
             vmem((ny, NX, HALF, LANES), bf16),
@@ -470,7 +481,7 @@
         out_shape=out_shape,
         in_specs=[pl.BlockSpec(memory_space=pl.ANY)] * 2,
         out_specs=(hbm,) * 2,
-        scratch_shapes=[dma((2,))],
+        scratch_shapes=[dma((5,))],
         compiler_params=pltpu.CompilerParams(vmem_limit_bytes=4 << 20),
         name="hand_over",
     )(*results)

time: 80 us -> 79.9 us (level)
  no operation moved by 1% of the time
where the time goes in v8:
time: 79.9 us; the launch traced here: 79.7 us
  Pallas kernels  78.3 us (98%)
    pallas_call x1, Pallas kernels, local(): pl.pallas_call(functools.partial(kernel, nz, ny), out_shape=out_shape, in...  77.4 us

profile of v8, /device:TPU:1, one launch (start us, length us, event | category | flops | bytes accessed | tf_op | source)
XLA Modules:
  0.0 79.7 jit_solution(4865770756219335133)
XLA Ops:
  0.6 0.0 copy-start
  0.6 0.7 copy-done
  1.4 77.4 %embed.1 = (f32[64,2048]{1,0:T(8,128)S(1)}, f32[64,64]{1,0:T(8,128)S(1)}) custom-call(f32[64,128]{1,0:T(8,128)S(1)} %copy-done, f32[64,2048]{1,0:T(8,128)} %bitcast.2), custom_call_target="tpu_custom_call" | custom-call | tf_op jit(solution)/shard_map/embed/pallas_call | solution.py:440
  78.8 0.8 %hand_over.1 = (f32[64,2048]{1,0:T(8,128)}, f32[64,64]{1,0:T(8,128)}) custom-call(f32[64,2048]{1,0:T(8,128)S(1)} %get-tuple-element.6.panels_ref, f32[64,64]{1,0:T(8,128)S(1)} %get-tuple-element.7.ritz_ref), custom_call_target="tpu_custom_call" | custom-call | tf_op jit(solution)/shard_map/hand_over/pallas_call | solution.py:479
Async XLA Ops:
  0.6 0.8 copy-start

commit v9 on v8

--- a/solution.py
+++ b/solution.py
@@ -100,7 +100,8 @@
     }
     axes["zc"] = (2 * nz, r, lambda p: (p, c))
     axes["other core"] = (nz, z, lambda p: (p * 2 + 1 - core, c))
-    beside = [lax.rem(y + step, ny) for step in ((1, ny - 1) if ny > 2 else range(1, ny))]
+    steps = (ny // 2, 1, ny - 1) if ny % 2 == 0 and ny > 2 else range(1, ny)
+    beside = [lax.rem(y + step, ny) for step in steps]
     for i, yy in enumerate(beside):
         axes[i] = (NX, x, lambda p, yy=yy: (r, yy * NX + p))
     met = ["xc", "y", "z", "other core", *range(len(beside))]
@@ -187,7 +188,7 @@
             return carry
 
         def on():
-            lax.fori_loop(1 + len(beside), ny, forward, 0)
+            lax.fori_loop(3, max(ny - 1, 3), forward, 0)
             for yy in beside:
                 wait(buf.at[yy, x], sems_y.at[yy])
             sent[slot + 1] = buf.at[:, pl.ds(0, NX - 1)]

time: 79.9 us -> 83.4 us (1.044)
  Pallas kernels: 78.3 us -> 81.8 us
    pallas_call x1, Pallas kernels: 77.4 us -> 81 us  [local(): pl.pallas_call(functools.partial(kernel, nz, ny), out_shape=out_shape, in...]
where the time goes in v9:
time: 83.4 us; the launch traced here: 83.2 us
  Pallas kernels  81.8 us (98%)
    pallas_call x1, Pallas kernels, local(): pl.pallas_call(functools.partial(kernel, nz, ny), out_shape=out_shape, in...  81 us

profile of v9, /device:TPU:1, one launch (start us, length us, event | category | flops | bytes accessed | tf_op | source)
XLA Modules:
  0.0 83.2 jit_solution(12076082344044823960)
XLA Ops:
  0.6 0.0 copy-start
  0.6 0.7 copy-done
  1.4 81.0 %embed.1 = (f32[64,2048]{1,0:T(8,128)S(1)}, f32[64,64]{1,0:T(8,128)S(1)}) custom-call(f32[64,128]{1,0:T(8,128)S(1)} %copy-done, f32[64,2048]{1,0:T(8,128)} %bitcast.2), custom_call_target="tpu_custom_call" | custom-call | tf_op jit(solution)/shard_map/embed/pallas_call | solution.py:441
  82.4 0.8 %hand_over.1 = (f32[64,2048]{1,0:T(8,128)}, f32[64,64]{1,0:T(8,128)}) custom-call(f32[64,2048]{1,0:T(8,128)S(1)} %get-tuple-element.6.panels_ref, f32[64,64]{1,0:T(8,128)S(1)} %get-tuple-element.7.ritz_ref), custom_call_target="tpu_custom_call" | custom-call | tf_op jit(solution)/shard_map/hand_over/pallas_call | solution.py:480
Async XLA Ops:
  0.6 0.8 copy-start

commit v10 on v8

--- a/solution.py
+++ b/solution.py
@@ -85,7 +85,7 @@
     nz, ny, points_ref, start_ref, out_ref, ritz_ref,
     points, pair_rows, pair_cols, start, rowpts, colpts, tile, colsum, deg, deg_zc, inv_col,
     laid_out, panel, send_p, recv_px, send_y, recv_py, scaled, total_c, half_c, recv_c, send_z, recv_z,
-    first_x, first_y, first_z, gram_x, gram_y, gram_z, ritz_x, ritz_y, ritz_z, whole, stack,
+    first_x, first_y, first_z, gram_x, gram_y, gram_z, ritz_x, ritz_y, ritz_z, gram_c, ritz_c, whole, stack,
     load_sem, points_sem, send_sem, recv_sem, from_y, from_x, part_x, again_y, again_x,
 ):
     r, c = lax.axis_index("row"), lax.axis_index("col")
@@ -379,9 +379,22 @@
     whole[y, x] = second_packed
     send(20, "y", lambda p: whole.at[y, x], whole.at[y, x], whole.at[pl.ds(0, ny - 1), 0])
     gram = all_sum(17, "xc", product_sums(second_packed, second_packed), gram_x)
-    ritz = all_sum(18, "z", product_sums(basis_packed, second_packed), ritz_z)
-    gram = all_sum(19, "y", gram(), gram_y)
-    ritz = all_sum(22, "xc", ritz(), ritz_x)
+    ritz = all_sum(22, "xc", product_sums(basis_packed, second_packed), ritz_x)
+
+    def my_half(value):
+        n = value.shape[0] // 2
+        return jnp.where(core == 0, value[:n], value[n:])
+
+    def join_halves(slot, value, buf):
+        buf[core] = value
+        send(slot, "c", lambda p: buf.at[core], buf.at[core], buf.at[0])
+
+        def done():
+            arrive(slot)
+            return jnp.concatenate([buf[0], buf[1]], axis=0)
+        return done
+    gram = all_sum(19, "y", my_half(gram()), gram_y)
+    ritz = all_sum(18, "z", my_half(ritz()), ritz_z)
     arrive(20)
     send(21, "x", lambda p: whole.at[:, x], whole.at[:, x], whole.at[:, pl.ds(0, NX - 1)])
     gram = all_sum(23, "z", gram(), gram_z)
@@ -398,12 +411,14 @@
         stack[:, columns] = jnp.concatenate([high, middle, low, high, middle, high], axis=0)
         return carry
     lax.fori_loop(0, ny, prepare, 0)
+    gram = join_halves(25, gram(), gram_c)
     last = inverse_factor(unpack(gram()) / total)
     high, middle, low = [part.astype(f32) for part in split(last, 3)]
     last = jnp.concatenate([high, high, high, middle, middle, low], axis=1).astype(bf16)
     block = min(4 * chunk, ny * chunk)
     for j in range(0, ny * chunk, block):
         out_ref[:, j:j + block] = dot(last, stack[:, j:j + block])
+    ritz = join_halves(26, ritz(), ritz_c)
     ritz_ref[...] = unpack(ritz()) / total
     drain()
 
@@ -433,6 +448,7 @@
     dma = pltpu.SemaphoreType.DMA
     hbm = pl.BlockSpec(memory_space=pltpu.HBM)
     sums = [vmem((n, vec // 2, 2 * vec), f32) for n in (2 * NX, ny, nz)]
+    second_sums = [sums[0], *[vmem((n, vec // 4, 2 * vec), f32) for n in (ny, nz)]]
     out_shape = (
         jax.ShapeDtypeStruct((vec, rows), f32),
         jax.ShapeDtypeStruct((vec, vec), f32),
@@ -466,10 +482,10 @@
             vmem((vec, ncols), f32),
             vmem((nz, HALF, LANES), f32),
             vmem((nz, HALF, LANES), f32),
-            *sums, *sums, *sums,
+            *sums, *second_sums, *second_sums, *[vmem((2, vec // 4, 2 * vec), f32)] * 2,
             vmem((ny, NX, HALF, LANES), f32),
             vmem((6 * vec, rows), bf16),
-            dma, dma, dma((25,)), dma((25,)), dma((ny,)), dma((ny,)), dma((ny,)), dma((ny,)), dma((ny,)),
+            dma, dma, dma((27,)), dma((27,)), dma((ny,)), dma((ny,)), dma((ny,)), dma((ny,)), dma((ny,)),
         ],
         compiler_params=pltpu.CompilerParams(
             collective_id=0, has_side_effects=True, vmem_limit_bytes=53 << 20

time: 79.9 us -> 81.4 us (1.019)
  Pallas kernels: 78.3 us -> 79.8 us
    pallas_call x1, Pallas kernels: 77.4 us -> 79 us  [local(): pl.pallas_call(functools.partial(kernel, nz, ny), out_shape=out_shape, in...]
where the time goes in v10:
time: 81.4 us; the launch traced here: 81.2 us
  Pallas kernels  79.8 us (98%)
    pallas_call x1, Pallas kernels, local(): pl.pallas_call(functools.partial(kernel, nz, ny), out_shape=out_shape, in...  79 us

profile of v10, /device:TPU:1, one launch (start us, length us, event | category | flops | bytes accessed | tf_op | source)
XLA Modules:
  0.0 81.2 jit_solution(18348714598902569899)
XLA Ops:
  0.6 0.0 copy-start
  0.6 0.7 copy-done
  1.4 79.0 %embed.1 = (f32[64,2048]{1,0:T(8,128)S(1)}, f32[64,64]{1,0:T(8,128)S(1)}) custom-call(f32[64,128]{1,0:T(8,128)S(1)} %copy-done, f32[64,2048]{1,0:T(8,128)} %bitcast.2), custom_call_target="tpu_custom_call" | custom-call | tf_op jit(solution)/shard_map/embed/pallas_call | solution.py:456
  80.4 0.8 %hand_over.1 = (f32[64,2048]{1,0:T(8,128)}, f32[64,64]{1,0:T(8,128)}) custom-call(f32[64,2048]{1,0:T(8,128)S(1)} %get-tuple-element.6.panels_ref, f32[64,64]{1,0:T(8,128)S(1)} %get-tuple-element.7.ritz_ref), custom_call_target="tpu_custom_call" | custom-call | tf_op jit(solution)/shard_map/hand_over/pallas_call | solution.py:495
Async XLA Ops:
  0.6 0.8 copy-start

commit v11 on v8

--- a/solution.py
+++ b/solution.py
@@ -100,10 +100,7 @@
     }
     axes["zc"] = (2 * nz, r, lambda p: (p, c))
     axes["other core"] = (nz, z, lambda p: (p * 2 + 1 - core, c))
-    beside = [lax.rem(y + step, ny) for step in ((1, ny - 1) if ny > 2 else range(1, ny))]
-    for i, yy in enumerate(beside):
-        axes[i] = (NX, x, lambda p, yy=yy: (r, yy * NX + p))
-    met = ["xc", "y", "z", "other core", *range(len(beside))]
+    met = ("xc", "y", "z", "other core")
     count = sum(axes[axis][0] - 1 for axis in met)
     chunk = NX * OWN
     mid = nz * HALF
@@ -175,9 +172,8 @@
     def spread(slot, buf, sems_y, sems_x):
         send(slot, "y", lambda p: buf.at[y, x], buf.at[y, x],
              buf.at[pl.ds(0, ny - 1), 0], sems_y.at[y])
-        for axis in ("x", *range(len(beside))):
-            send(slot + 1, axis, lambda p: buf.at[y, x], buf.at[y, x],
-                 buf.at[:, pl.ds(0, NX - 1)], sems_x.at[y])
+        send(slot + 1, "x", lambda p: buf.at[y, x], buf.at[y, x],
+             buf.at[:, pl.ds(0, NX - 1)], sems_x.at[y])
 
         def forward(i, carry):
             yy = near(i)
@@ -187,9 +183,7 @@
             return carry
 
         def on():
-            lax.fori_loop(1 + len(beside), ny, forward, 0)
-            for yy in beside:
-                wait(buf.at[yy, x], sems_y.at[yy])
+            lax.fori_loop(1, ny, forward, 0)
             sent[slot + 1] = buf.at[:, pl.ds(0, NX - 1)]
         return on
 

time: 79.9 us -> 82 us (1.026)
  Pallas kernels: 78.3 us -> 80.4 us
    pallas_call x1, Pallas kernels: 77.4 us -> 79.5 us  [local(): pl.pallas_call(functools.partial(kernel, nz, ny), out_shape=out_shape, in...]
where the time goes in v11:
time: 82 us; the launch traced here: 81.8 us
  Pallas kernels  80.4 us (98%)
    pallas_call x1, Pallas kernels, local(): pl.pallas_call(functools.partial(kernel, nz, ny), out_shape=out_shape, in...  79.5 us

profile of v11, /device:TPU:1, one launch (start us, length us, event | category | flops | bytes accessed | tf_op | source)
XLA Modules:
  0.0 81.8 jit_solution(10322420709397461272)
XLA Ops:
  0.6 0.0 copy-start
  0.6 0.7 copy-done
  1.4 79.5 %embed.1 = (f32[64,2048]{1,0:T(8,128)S(1)}, f32[64,64]{1,0:T(8,128)S(1)}) custom-call(f32[64,128]{1,0:T(8,128)S(1)} %copy-done, f32[64,2048]{1,0:T(8,128)} %bitcast.2), custom_call_target="tpu_custom_call" | custom-call | tf_op jit(solution)/shard_map/embed/pallas_call | solution.py:434
  80.9 0.8 %hand_over.1 = (f32[64,2048]{1,0:T(8,128)}, f32[64,64]{1,0:T(8,128)}) custom-call(f32[64,2048]{1,0:T(8,128)S(1)} %get-tuple-element.6.panels_ref, f32[64,64]{1,0:T(8,128)S(1)} %get-tuple-element.7.ritz_ref), custom_call_target="tpu_custom_call" | custom-call | tf_op jit(solution)/shard_map/hand_over/pallas_call | solution.py:473
Async XLA Ops:
  0.6 0.8 copy-start
